TPU v7x, 256 devices: a whole 4x4x8 slice. The times are simulated.
256 devices in a mesh: stream: 32 (over x, y, core), normal: 8 (over z).
Axes of the slice: x: 4, y: 4, z: 8, core: 2. Of those that a mesh axis runs over, the one named last changes fastest.
Arguments:
- state: float32 [5, 128, 128, 128], P(None, 'stream', 'normal'), may hold values from -2 to 6.5, as said below
- viscosity: float32 [128, 128, 128], P('stream', 'normal'), may hold values from 200 to 1600
- residual_other: float32 [5, 128, 128, 128], P(None, 'stream', 'normal'), may hold values from -2402 to 2402
Outputs:
- increment: float32 [5, 128, 128, 128], P(None, 'stream', 'normal')
Inputs may be any that keep to these rules, and one draw needn't show every extreme that they name: `state`: the conserved variables of a gas with gamma 1.4: density between 0.5 and 2, pressure between 0.5 and 2, streamwise speed at most 1 and the other speeds at most 0.5 in magnitude.
All inputs are finite; a program needn't handle non-finite values.
Results may differ from a plain program's by a relative error of at most 0.0003.
Values sent between devices are 32-bit elements; how exact they have to be, the bound alone decides.
A program may use at most 128 MiB of HBM per device.

v0:
```python
import jax
import jax.numpy as jnp
from jax import lax
from jax.sharding import PartitionSpec as P

GAMMA = 1.4
GM_ONE = 0.4
STREAM_STEP = 1.0
NORMAL_STEP = 40.0
SMOOTHING = 8.0


def padded_2(cells, sides, width):
    for axis, dim in sides:
        count = lax.axis_size(axis)
        ends = count - 1
        head = lax.slice_in_dim(cells, 0, width, axis=dim)
        tail = lax.slice_in_dim(cells, cells.shape[dim] - width, cells.shape[dim], axis=dim)
        cells = jnp.concatenate(
            [
                lax.ppermute(tail, axis, [(i, (i + 1) % count) for i in range(ends)]),
                cells,
                lax.ppermute(head, axis, [((i + 1) % count, i) for i in range(ends)]),
            ],
            axis=dim,
        )
    return cells


def shifted(block, axis, distance):
    devices = range(lax.axis_size(axis))
    route = [(i - distance, i) for i in devices if i - distance in devices]
    return lax.ppermute(block, axis, route)


def stream_jacobian(state):
    rho, mom_x, mom_y, mom_z, energy = (state[0], state[1], state[2], state[3], state[4])
    speed_u = mom_x / rho
    speed_v = mom_y / rho
    speed_w = mom_z / rho
    square = speed_u * speed_u + speed_v * speed_v + speed_w * speed_w
    pressure = GM_ONE * (energy - 0.5 * rho * square)
    enthalpy = (energy + pressure) / rho
    half = 0.5 * GM_ONE * square
    zero = jnp.zeros_like(speed_u)
    unity = jnp.ones_like(speed_u)
    rows_list = [
        [zero, unity, zero, zero, zero],
        [
            half - speed_u * speed_u,
            (3.0 - GAMMA) * speed_u,
            -GM_ONE * speed_v,
            -GM_ONE * speed_w,
            GM_ONE * unity,
        ],
        [-speed_u * speed_v, speed_v, speed_u, zero, zero],
        [-speed_u * speed_w, speed_w, zero, speed_u, zero],
        [
            speed_u * (half - enthalpy),
            enthalpy - GM_ONE * speed_u * speed_u,
            -GM_ONE * speed_u * speed_v,
            -GM_ONE * speed_u * speed_w,
            GAMMA * speed_u,
        ],
    ]
    return jnp.stack([jnp.stack(row_items) for row_items in rows_list])


def normal_flux(state):
    rho, mom_x, mom_y, mom_z, energy = (state[0], state[1], state[2], state[3], state[4])
    pressure = GM_ONE * (energy - 0.5 * (mom_x * mom_x + mom_y * mom_y + mom_z * mom_z) / rho)
    speed_v = mom_y / rho
    return jnp.stack(
        [
            mom_y,
            mom_x * speed_v,
            mom_y * speed_v + pressure,
            mom_z * speed_v,
            (energy + pressure) * speed_v,
        ]
    )


def mat_mul(left, right):
    return jnp.sum(left[:, :, None] * right[None], axis=1)


def solve_five(matrix, right):
    rows_m = [matrix[r] for r in range(5)]
    rows_b = [right[r] for r in range(5)]
    for pivot in range(5):
        factor = 1.0 / rows_m[pivot][pivot]
        rows_m[pivot] = rows_m[pivot] * factor[None]
        rows_b[pivot] = rows_b[pivot] * factor[None]
        for other in range(5):
            if other != pivot:
                weight = rows_m[other][pivot]
                rows_m[other] = rows_m[other] - weight[None] * rows_m[pivot]
                rows_b[other] = rows_b[other] - weight[None] * rows_b[pivot]
    return jnp.stack(rows_b)


def join_prefix(pre_g, pre_b, own):
    gf, af, bf, gl, al, bl = own
    eye = jnp.eye(5, dtype=jnp.float32)[:, :, None, None]
    sol = solve_five(
        eye - mat_mul(pre_b, af),
        jnp.concatenate([pre_g + mat_mul(pre_b, gf), mat_mul(pre_b, bf)], axis=1),
    )
    return (gl + mat_mul(al, sol[:, 0:1]), bl + mat_mul(al, sol[:, 1:6]))


def join_suffix(own, suf_g, suf_c):
    gf, af, bf, gl, al, bl = own
    eye = jnp.eye(5, dtype=jnp.float32)[:, :, None, None]
    sol = solve_five(
        eye - mat_mul(suf_c, bl),
        jnp.concatenate([suf_g + mat_mul(suf_c, gl), mat_mul(suf_c, al)], axis=1),
    )
    return (gf + mat_mul(bf, sol[:, 0:1]), af + mat_mul(bf, sol[:, 1:6]))


def on_device(state, viscosity, residual_other):
    flux = normal_flux(state)
    padded = padded_2(jnp.concatenate([state, flux], axis=0), (("normal", 2),), 2)
    count = state.shape[2]

    def planes(shift):
        return padded[:, :, 2 + shift : 2 + shift + count]

    qs = {s: planes(s)[:5] for s in (-2, -1, 0, 1, 2)}
    rhs = (
        residual_other
        - NORMAL_STEP * (planes(1)[5:] - planes(-1)[5:])
        + viscosity[None] * (qs[1] - 2.0 * qs[0] + qs[-1])
        - SMOOTHING * (qs[2] - 4.0 * qs[1] + 6.0 * qs[0] - 4.0 * qs[-1] + qs[-2])
    )
    jac_pad = padded_2(stream_jacobian(state), (("stream", 2),), 1)
    cells = state.shape[1]
    grid_lines = (state.shape[2], state.shape[3])
    eye_cells = jnp.eye(5, dtype=jnp.float32)[:, :, None, None, None]
    lower_blocks = jnp.moveaxis(-STREAM_STEP * jac_pad[:, :, :-2] - viscosity * eye_cells, 2, 0)
    upper_blocks = jnp.moveaxis(STREAM_STEP * jac_pad[:, :, 2:] - viscosity * eye_cells, 2, 0)
    diagonal_blocks = jnp.moveaxis((1.0 + 2.0 * viscosity) * eye_cells, 2, 0)
    rhs_cells = jnp.moveaxis(rhs, 1, 0)[:, :, None]
    left_cols = jnp.zeros_like(lower_blocks).at[0].set(-lower_blocks[0])
    right_cols = jnp.zeros_like(upper_blocks).at[cells - 1].set(-upper_blocks[cells - 1])
    forcing_vector = jnp.concatenate([rhs_cells, left_cols, right_cols], axis=2)

    def forward_elimination(carry, item):
        e_prev, y_prev = carry
        low, up, dia, source_term = item
        work = dia - mat_mul(low, e_prev)
        sol = solve_five(work, jnp.concatenate([up, source_term - mat_mul(low, y_prev)], axis=1))
        return ((sol[:, :5], sol[:, 5:]), (sol[:, :5], sol[:, 5:]))

    start_index = (
        jnp.zeros((5, 5) + grid_lines, jnp.float32),
        jnp.zeros((5, 11) + grid_lines, jnp.float32),
    )
    unused_slot, (elimination_factor, partial_solution) = lax.scan(
        forward_elimination,
        start_index,
        (lower_blocks, upper_blocks, diagonal_blocks, forcing_vector),
    )

    def backward_substitution(x_next, item):
        e_now, y_now = item
        x_now = y_now - mat_mul(e_now, x_next)
        return (x_now, x_now)

    unused_slot, local = lax.scan(
        backward_substitution,
        jnp.zeros((5, 11) + grid_lines, jnp.float32),
        (elimination_factor, partial_solution),
        reverse=True,
    )
    first = local[0]
    final = local[cells - 1]
    own = (
        first[:, 0:1],
        first[:, 1:6],
        first[:, 6:11],
        final[:, 0:1],
        final[:, 1:6],
        final[:, 6:11],
    )
    zero_pack = jnp.zeros((5, 6) + grid_lines, jnp.float32)

    def relay(step, carry):
        out_pre, out_suf, old_pre, old_suf = carry
        inc_pre = shifted(out_pre, "stream", 1)
        inc_suf = shifted(out_suf, "stream", -1)
        last_g, last_b = join_prefix(inc_pre[:, 0:1], inc_pre[:, 1:6], own)
        first_g, first_a = join_suffix(own, inc_suf[:, 0:1], inc_suf[:, 1:6])
        return (
            jnp.concatenate([last_g, last_b], axis=1),
            jnp.concatenate([first_g, first_a], axis=1),
            inc_pre,
            inc_suf,
        )

    begin = (
        jnp.concatenate([own[3], own[5]], axis=1),
        jnp.concatenate([own[0], own[1]], axis=1),
        zero_pack,
        zero_pack,
    )
    out_pre, out_suf, inc_pre, inc_suf = lax.fori_loop(0, lax.axis_size("stream") - 1, relay, begin)
    pre_g, pre_b = (inc_pre[:, 0:1], inc_pre[:, 1:6])
    suf_g, suf_c = (inc_suf[:, 0:1], inc_suf[:, 1:6])
    last_g, last_b = (out_pre[:, 0:1], out_pre[:, 1:6])
    first_g, first_a = (out_suf[:, 0:1], out_suf[:, 1:6])
    eye = jnp.eye(5, dtype=jnp.float32)[:, :, None, None]
    last_value = solve_five(eye - mat_mul(last_b, suf_c), last_g + mat_mul(last_b, suf_g))
    right_value = suf_g + mat_mul(suf_c, last_value)
    left_value = solve_five(eye - mat_mul(pre_b, first_a), pre_g + mat_mul(pre_b, first_g))
    increment = (
        local[:, :, 0]
        + jnp.sum(local[:, :, 1:6] * left_value[None, None, :, 0], axis=2)
        + jnp.sum(local[:, :, 6:11] * right_value[None, None, :, 0], axis=2)
    )
    return jnp.moveaxis(increment, 0, 1)


def solution(mesh):
    placed = (
        P(None, "stream", "normal", None),
        P("stream", "normal", None),
        P(None, "stream", "normal", None),
    )
    return jax.shard_map(
        on_device,
        mesh=mesh,
        in_specs=placed,
        out_specs=P(None, "stream", "normal", None),
        check_vma=False,
    )
```

profile of v0, /device:TPU:102, one launch (start us, length us, event | category | flops | bytes accessed | tf_op | source)
XLA Modules:
  0.0 461.1 jit_solution(6452371194387444413)
XLA Ops:
  3.2 5.0 %collective-permute-start.4 = (f32[10,4,2,128]{3,2,0,1:T(2,128)S(1)}, f32[10,4,2,128]{3,2,0,1:T(2,128)S(1)}, u32[]{:S(2)}, u32[]{:S(2)}) collective-permute-start(f32[10,4,2,128]{3,2,0,1:T(2,128)S(1)} %get-tuple-element.513), channel_id=1, source_target_pairs={{0,1},{1,2},{2,3},{3,4},{4,5},{5,6},{6,7},{8,9},{9,10},{10,11},{11... | collective-permute-start | bytes 122888 | tf_op jit(solution)/shard_map/ppermute | solution.py:21
  8.7 4.3 collective-permute-start.2
  16.2 5.9 %collective-permute-done.5 = f32[5,5,1,16,128]{4,3,1,2,0:T(8,128)S(1)} collective-permute-done((f32[5,5,1,16,128]{4,3,1,2,0:T(8,128)S(1)}, f32[5,5,1,16,128]{4,3,1,2,0:T(8,128)S(1)}, u32[]{:S(2)}, u32[]{:S(2)}) %collective-permute-start.5) | collective-permute-done | bytes 204832 | tf_op jit(solution)/shard_map/ppermute | solution.py:21
  25.9 19.3 %while.51 = (s32[]{:T(128)}, f32[5,5,16,128]{3,2,1,0:T(8,128)S(1)}, f32[5,11,16,128]{3,2,1,0:T(8,128)S(1)}, f32[4,5,5,16,128]{4,3,2,1,0:T(8,128)}, f32[4,5,11,16...) while((s32[]{:T(128)}, f32[5,5,16,128]{3,2,1,0:T(8,128)S(1)}, ...), condition=%wide.region_3.4_spmd, body=%wide.region_0.3_spmd.sunk | while | flops 3590145 | bytes 11829877 | solution.py:161
  46.6 8.4 %while.53 = (s32[]{:T(128)}, f32[5,11,16,128]{3,2,1,0:T(8,128)S(1)}, f32[4,5,11,16,128]{4,3,2,1,0:T(8,128)}, f32[4,5,11,16,128]{4,3,2,1,0:T(8,128)S(1)}, f32[4,5...) while((s32[]{:T(128)}, f32[5,11,16,128]{3,2,1,0:T(8,128)S(1)}, ...), condition=%wide.region_6.7_spmd.clone, body=%wide.region_4.0_spmd.clone.sunk | while | flops 1351684 | bytes 5120119 | solution.py:172
  56.4 396.5 %while.52 = (s32[]{:T(128)}, f32[5,6,16,128]{3,2,1,0:T(8,128)S(1)}, f32[5,6,16,128]{3,2,1,0:T(8,128)S(1)}, f32[5,6,16,128]{3,2,1,0:T(8,128)}, f32[5,6,16,128]{3,...) while((s32[]{:T(128)}, f32[5,6,16,128]{3,2,1,0:T(8,128)S(1)}, ...), condition=%wide.region_18.19_spmd, body=%wide.region_7.18_spmd.sunk | while | flops 5357618 | bytes 19849768 | solution.py:209
  62.9 5.0 %collective-permute-done.1 = f32[5,6,16,128]{3,2,1,0:T(8,128)S(1)} collective-permute-done((f32[5,6,16,128]{3,2,1,0:T(8,128)S(1)}, f32[5,6,16,128]{3,2,1,0:T(8,128)S(1)}, u32[]{:S(2)}, u32[]{:S(2)}) %collective-permute-start.1) | collective-permute-done | bytes 245792 | tf_op jit(solution)/shard_map/while/body/eval_jaxpr/ppermute | solution.py:33
  71.1 2.4 collective-permute-start.1
  75.7 5.0 %collective-permute-done.1 = f32[5,6,16,128]{3,2,1,0:T(8,128)S(1)} collective-permute-done((f32[5,6,16,128]{3,2,1,0:T(8,128)S(1)}, f32[5,6,16,128]{3,2,1,0:T(8,128)S(1)}, u32[]{:S(2)}, u32[]{:S(2)}) %collective-permute-start.1) | collective-permute-done | bytes 245792 | tf_op jit(solution)/shard_map/while/body/eval_jaxpr/ppermute | solution.py:33
  83.9 2.4 collective-permute-start.1
  88.5 5.0 %collective-permute-done.1 = f32[5,6,16,128]{3,2,1,0:T(8,128)S(1)} collective-permute-done((f32[5,6,16,128]{3,2,1,0:T(8,128)S(1)}, f32[5,6,16,128]{3,2,1,0:T(8,128)S(1)}, u32[]{:S(2)}, u32[]{:S(2)}) %collective-permute-start.1) | collective-permute-done | bytes 245792 | tf_op jit(solution)/shard_map/while/body/eval_jaxpr/ppermute | solution.py:33
  96.7 2.4 collective-permute-start.1
  101.3 5.0 %collective-permute-done.1 = f32[5,6,16,128]{3,2,1,0:T(8,128)S(1)} collective-permute-done((f32[5,6,16,128]{3,2,1,0:T(8,128)S(1)}, f32[5,6,16,128]{3,2,1,0:T(8,128)S(1)}, u32[]{:S(2)}, u32[]{:S(2)}) %collective-permute-start.1) | collective-permute-done | bytes 245792 | tf_op jit(solution)/shard_map/while/body/eval_jaxpr/ppermute | solution.py:33
  109.5 2.4 collective-permute-start.1
  114.1 5.0 %collective-permute-done.1 = f32[5,6,16,128]{3,2,1,0:T(8,128)S(1)} collective-permute-done((f32[5,6,16,128]{3,2,1,0:T(8,128)S(1)}, f32[5,6,16,128]{3,2,1,0:T(8,128)S(1)}, u32[]{:S(2)}, u32[]{:S(2)}) %collective-permute-start.1) | collective-permute-done | bytes 245792 | tf_op jit(solution)/shard_map/while/body/eval_jaxpr/ppermute | solution.py:33
  126.9 5.0 %collective-permute-done.1 = f32[5,6,16,128]{3,2,1,0:T(8,128)S(1)} collective-permute-done((f32[5,6,16,128]{3,2,1,0:T(8,128)S(1)}, f32[5,6,16,128]{3,2,1,0:T(8,128)S(1)}, u32[]{:S(2)}, u32[]{:S(2)}) %collective-permute-start.1) | collective-permute-done | bytes 245792 | tf_op jit(solution)/shard_map/while/body/eval_jaxpr/ppermute | solution.py:33
  135.0 2.4 collective-permute-start.1
  139.6 5.0 %collective-permute-done.1 = f32[5,6,16,128]{3,2,1,0:T(8,128)S(1)} collective-permute-done((f32[5,6,16,128]{3,2,1,0:T(8,128)S(1)}, f32[5,6,16,128]{3,2,1,0:T(8,128)S(1)}, u32[]{:S(2)}, u32[]{:S(2)}) %collective-permute-start.1) | collective-permute-done | bytes 245792 | tf_op jit(solution)/shard_map/while/body/eval_jaxpr/ppermute | solution.py:33
  147.8 2.4 collective-permute-start.1
  152.4 5.0 %collective-permute-done.1 = f32[5,6,16,128]{3,2,1,0:T(8,128)S(1)} collective-permute-done((f32[5,6,16,128]{3,2,1,0:T(8,128)S(1)}, f32[5,6,16,128]{3,2,1,0:T(8,128)S(1)}, u32[]{:S(2)}, u32[]{:S(2)}) %collective-permute-start.1) | collective-permute-done | bytes 245792 | tf_op jit(solution)/shard_map/while/body/eval_jaxpr/ppermute | solution.py:33
  165.2 5.0 %collective-permute-done.1 = f32[5,6,16,128]{3,2,1,0:T(8,128)S(1)} collective-permute-done((f32[5,6,16,128]{3,2,1,0:T(8,128)S(1)}, f32[5,6,16,128]{3,2,1,0:T(8,128)S(1)}, u32[]{:S(2)}, u32[]{:S(2)}) %collective-permute-start.1) | collective-permute-done | bytes 245792 | tf_op jit(solution)/shard_map/while/body/eval_jaxpr/ppermute | solution.py:33
  173.4 2.4 collective-permute-start.1
  178.0 5.0 %collective-permute-done.1 = f32[5,6,16,128]{3,2,1,0:T(8,128)S(1)} collective-permute-done((f32[5,6,16,128]{3,2,1,0:T(8,128)S(1)}, f32[5,6,16,128]{3,2,1,0:T(8,128)S(1)}, u32[]{:S(2)}, u32[]{:S(2)}) %collective-permute-start.1) | collective-permute-done | bytes 245792 | tf_op jit(solution)/shard_map/while/body/eval_jaxpr/ppermute | solution.py:33
  186.2 2.4 collective-permute-start.1
  190.8 5.0 %collective-permute-done.1 = f32[5,6,16,128]{3,2,1,0:T(8,128)S(1)} collective-permute-done((f32[5,6,16,128]{3,2,1,0:T(8,128)S(1)}, f32[5,6,16,128]{3,2,1,0:T(8,128)S(1)}, u32[]{:S(2)}, u32[]{:S(2)}) %collective-permute-start.1) | collective-permute-done | bytes 245792 | tf_op jit(solution)/shard_map/while/body/eval_jaxpr/ppermute | solution.py:33
  199.0 2.4 collective-permute-start.1
  203.6 5.0 %collective-permute-done.1 = f32[5,6,16,128]{3,2,1,0:T(8,128)S(1)} collective-permute-done((f32[5,6,16,128]{3,2,1,0:T(8,128)S(1)}, f32[5,6,16,128]{3,2,1,0:T(8,128)S(1)}, u32[]{:S(2)}, u32[]{:S(2)}) %collective-permute-start.1) | collective-permute-done | bytes 245792 | tf_op jit(solution)/shard_map/while/body/eval_jaxpr/ppermute | solution.py:33
  211.8 2.4 collective-permute-start.1
  216.4 5.0 %collective-permute-done.1 = f32[5,6,16,128]{3,2,1,0:T(8,128)S(1)} collective-permute-done((f32[5,6,16,128]{3,2,1,0:T(8,128)S(1)}, f32[5,6,16,128]{3,2,1,0:T(8,128)S(1)}, u32[]{:S(2)}, u32[]{:S(2)}) %collective-permute-start.1) | collective-permute-done | bytes 245792 | tf_op jit(solution)/shard_map/while/body/eval_jaxpr/ppermute | solution.py:33
  224.6 2.4 collective-permute-start.1
  229.2 5.0 %collective-permute-done.1 = f32[5,6,16,128]{3,2,1,0:T(8,128)S(1)} collective-permute-done((f32[5,6,16,128]{3,2,1,0:T(8,128)S(1)}, f32[5,6,16,128]{3,2,1,0:T(8,128)S(1)}, u32[]{:S(2)}, u32[]{:S(2)}) %collective-permute-start.1) | collective-permute-done | bytes 245792 | tf_op jit(solution)/shard_map/while/body/eval_jaxpr/ppermute | solution.py:33
  242.0 5.0 %collective-permute-done.1 = f32[5,6,16,128]{3,2,1,0:T(8,128)S(1)} collective-permute-done((f32[5,6,16,128]{3,2,1,0:T(8,128)S(1)}, f32[5,6,16,128]{3,2,1,0:T(8,128)S(1)}, u32[]{:S(2)}, u32[]{:S(2)}) %collective-permute-start.1) | collective-permute-done | bytes 245792 | tf_op jit(solution)/shard_map/while/body/eval_jaxpr/ppermute | solution.py:33
  254.7 5.0 %collective-permute-done.1 = f32[5,6,16,128]{3,2,1,0:T(8,128)S(1)} collective-permute-done((f32[5,6,16,128]{3,2,1,0:T(8,128)S(1)}, f32[5,6,16,128]{3,2,1,0:T(8,128)S(1)}, u32[]{:S(2)}, u32[]{:S(2)}) %collective-permute-start.1) | collective-permute-done | bytes 245792 | tf_op jit(solution)/shard_map/while/body/eval_jaxpr/ppermute | solution.py:33
  267.5 5.0 %collective-permute-done.1 = f32[5,6,16,128]{3,2,1,0:T(8,128)S(1)} collective-permute-done((f32[5,6,16,128]{3,2,1,0:T(8,128)S(1)}, f32[5,6,16,128]{3,2,1,0:T(8,128)S(1)}, u32[]{:S(2)}, u32[]{:S(2)}) %collective-permute-start.1) | collective-permute-done | bytes 245792 | tf_op jit(solution)/shard_map/while/body/eval_jaxpr/ppermute | solution.py:33
  280.3 5.0 %collective-permute-done.1 = f32[5,6,16,128]{3,2,1,0:T(8,128)S(1)} collective-permute-done((f32[5,6,16,128]{3,2,1,0:T(8,128)S(1)}, f32[5,6,16,128]{3,2,1,0:T(8,128)S(1)}, u32[]{:S(2)}, u32[]{:S(2)}) %collective-permute-start.1) | collective-permute-done | bytes 245792 | tf_op jit(solution)/shard_map/while/body/eval_jaxpr/ppermute | solution.py:33
  293.1 5.0 %collective-permute-done.1 = f32[5,6,16,128]{3,2,1,0:T(8,128)S(1)} collective-permute-done((f32[5,6,16,128]{3,2,1,0:T(8,128)S(1)}, f32[5,6,16,128]{3,2,1,0:T(8,128)S(1)}, u32[]{:S(2)}, u32[]{:S(2)}) %collective-permute-start.1) | collective-permute-done | bytes 245792 | tf_op jit(solution)/shard_map/while/body/eval_jaxpr/ppermute | solution.py:33
  305.9 5.0 %collective-permute-done.1 = f32[5,6,16,128]{3,2,1,0:T(8,128)S(1)} collective-permute-done((f32[5,6,16,128]{3,2,1,0:T(8,128)S(1)}, f32[5,6,16,128]{3,2,1,0:T(8,128)S(1)}, u32[]{:S(2)}, u32[]{:S(2)}) %collective-permute-start.1) | collective-permute-done | bytes 245792 | tf_op jit(solution)/shard_map/while/body/eval_jaxpr/ppermute | solution.py:33
  318.7 5.0 %collective-permute-done.1 = f32[5,6,16,128]{3,2,1,0:T(8,128)S(1)} collective-permute-done((f32[5,6,16,128]{3,2,1,0:T(8,128)S(1)}, f32[5,6,16,128]{3,2,1,0:T(8,128)S(1)}, u32[]{:S(2)}, u32[]{:S(2)}) %collective-permute-start.1) | collective-permute-done | bytes 245792 | tf_op jit(solution)/shard_map/while/body/eval_jaxpr/ppermute | solution.py:33
  331.5 5.0 %collective-permute-done.1 = f32[5,6,16,128]{3,2,1,0:T(8,128)S(1)} collective-permute-done((f32[5,6,16,128]{3,2,1,0:T(8,128)S(1)}, f32[5,6,16,128]{3,2,1,0:T(8,128)S(1)}, u32[]{:S(2)}, u32[]{:S(2)}) %collective-permute-start.1) | collective-permute-done | bytes 245792 | tf_op jit(solution)/shard_map/while/body/eval_jaxpr/ppermute | solution.py:33
  344.3 5.0 %collective-permute-done.1 = f32[5,6,16,128]{3,2,1,0:T(8,128)S(1)} collective-permute-done((f32[5,6,16,128]{3,2,1,0:T(8,128)S(1)}, f32[5,6,16,128]{3,2,1,0:T(8,128)S(1)}, u32[]{:S(2)}, u32[]{:S(2)}) %collective-permute-start.1) | collective-permute-done | bytes 245792 | tf_op jit(solution)/shard_map/while/body/eval_jaxpr/ppermute | solution.py:33
  357.1 5.0 %collective-permute-done.1 = f32[5,6,16,128]{3,2,1,0:T(8,128)S(1)} collective-permute-done((f32[5,6,16,128]{3,2,1,0:T(8,128)S(1)}, f32[5,6,16,128]{3,2,1,0:T(8,128)S(1)}, u32[]{:S(2)}, u32[]{:S(2)}) %collective-permute-start.1) | collective-permute-done | bytes 245792 | tf_op jit(solution)/shard_map/while/body/eval_jaxpr/ppermute | solution.py:33
  369.8 5.0 %collective-permute-done.1 = f32[5,6,16,128]{3,2,1,0:T(8,128)S(1)} collective-permute-done((f32[5,6,16,128]{3,2,1,0:T(8,128)S(1)}, f32[5,6,16,128]{3,2,1,0:T(8,128)S(1)}, u32[]{:S(2)}, u32[]{:S(2)}) %collective-permute-start.1) | collective-permute-done | bytes 245792 | tf_op jit(solution)/shard_map/while/body/eval_jaxpr/ppermute | solution.py:33
  382.6 5.0 %collective-permute-done.1 = f32[5,6,16,128]{3,2,1,0:T(8,128)S(1)} collective-permute-done((f32[5,6,16,128]{3,2,1,0:T(8,128)S(1)}, f32[5,6,16,128]{3,2,1,0:T(8,128)S(1)}, u32[]{:S(2)}, u32[]{:S(2)}) %collective-permute-start.1) | collective-permute-done | bytes 245792 | tf_op jit(solution)/shard_map/while/body/eval_jaxpr/ppermute | solution.py:33
  395.4 5.0 %collective-permute-done.1 = f32[5,6,16,128]{3,2,1,0:T(8,128)S(1)} collective-permute-done((f32[5,6,16,128]{3,2,1,0:T(8,128)S(1)}, f32[5,6,16,128]{3,2,1,0:T(8,128)S(1)}, u32[]{:S(2)}, u32[]{:S(2)}) %collective-permute-start.1) | collective-permute-done | bytes 245792 | tf_op jit(solution)/shard_map/while/body/eval_jaxpr/ppermute | solution.py:33
  408.2 5.0 %collective-permute-done.1 = f32[5,6,16,128]{3,2,1,0:T(8,128)S(1)} collective-permute-done((f32[5,6,16,128]{3,2,1,0:T(8,128)S(1)}, f32[5,6,16,128]{3,2,1,0:T(8,128)S(1)}, u32[]{:S(2)}, u32[]{:S(2)}) %collective-permute-start.1) | collective-permute-done | bytes 245792 | tf_op jit(solution)/shard_map/while/body/eval_jaxpr/ppermute | solution.py:33
  421.0 5.0 %collective-permute-done.1 = f32[5,6,16,128]{3,2,1,0:T(8,128)S(1)} collective-permute-done((f32[5,6,16,128]{3,2,1,0:T(8,128)S(1)}, f32[5,6,16,128]{3,2,1,0:T(8,128)S(1)}, u32[]{:S(2)}, u32[]{:S(2)}) %collective-permute-start.1) | collective-permute-done | bytes 245792 | tf_op jit(solution)/shard_map/while/body/eval_jaxpr/ppermute | solution.py:33
  433.8 5.0 %collective-permute-done.1 = f32[5,6,16,128]{3,2,1,0:T(8,128)S(1)} collective-permute-done((f32[5,6,16,128]{3,2,1,0:T(8,128)S(1)}, f32[5,6,16,128]{3,2,1,0:T(8,128)S(1)}, u32[]{:S(2)}, u32[]{:S(2)}) %collective-permute-start.1) | collective-permute-done | bytes 245792 | tf_op jit(solution)/shard_map/while/body/eval_jaxpr/ppermute | solution.py:33
  446.6 5.0 %collective-permute-done.1 = f32[5,6,16,128]{3,2,1,0:T(8,128)S(1)} collective-permute-done((f32[5,6,16,128]{3,2,1,0:T(8,128)S(1)}, f32[5,6,16,128]{3,2,1,0:T(8,128)S(1)}, u32[]{:S(2)}, u32[]{:S(2)}) %collective-permute-start.1) | collective-permute-done | bytes 245792 | tf_op jit(solution)/shard_map/while/body/eval_jaxpr/ppermute | solution.py:33
  (2926 shorter events, 244.3 us)
Async XLA Ops:
  1.1 14.8 %collective-permute-start.3 = (f32[10,4,2,128]{3,2,0,1:T(2,128)S(1)}, f32[10,4,2,128]{3,2,0,1:T(2,128)S(1)}, u32[]{:S(2)}, u32[]{:S(2)}) collective-permute-start(f32[10,4,2,128]{3,2,0,1:T(2,128)S(1)} %get-tuple-element.512), channel_id=1, source_target_pairs={{1,0},{2,1},{3,2},{4,3},{5,4},{6,5},{7,6},{9,8},{10,9},{11,10},{12... | collective-permute-start | bytes 122888 | tf_op jit(solution)/shard_map/ppermute | solution.py:23
  3.2 12.8 %collective-permute-start.4 = (f32[10,4,2,128]{3,2,0,1:T(2,128)S(1)}, f32[10,4,2,128]{3,2,0,1:T(2,128)S(1)}, u32[]{:S(2)}, u32[]{:S(2)}) collective-permute-start(f32[10,4,2,128]{3,2,0,1:T(2,128)S(1)} %get-tuple-element.513), channel_id=1, source_target_pairs={{0,1},{1,2},{2,3},{3,4},{4,5},{5,6},{6,7},{8,9},{9,10},{10,11},{11... | collective-permute-start | bytes 122888 | tf_op jit(solution)/shard_map/ppermute | solution.py:21
  8.7 7.5 %collective-permute-start.2 = (f32[5,5,1,16,128]{4,3,1,2,0:T(8,128)S(1)}, f32[5,5,1,16,128]{4,3,1,2,0:T(8,128)S(1)}, u32[]{:S(2)}, u32[]{:S(2)}) collective-permute-start(f32[5,5,1,16,128]{4,3,1,2,0:T(8,128)S(1)} %get-tuple-element.507), channel_id=1, source_target_pairs={{8,0},{16,8},{24,16},{32,24},{40,32},{48,40},{56,48},{64,56},{72,6... | collective-permute-start | bytes 614408 | tf_op jit(solution)/shard_map/ppermute | solution.py:23
  13.0 9.2 %collective-permute-start.5 = (f32[5,5,1,16,128]{4,3,1,2,0:T(8,128)S(1)}, f32[5,5,1,16,128]{4,3,1,2,0:T(8,128)S(1)}, u32[]{:S(2)}, u32[]{:S(2)}) collective-permute-start(f32[5,5,1,16,128]{4,3,1,2,0:T(8,128)S(1)} %get-tuple-element.506), channel_id=1, source_target_pairs={{0,8},{8,16},{16,24},{24,32},{32,40},{40,48},{48,56},{56,64},{64,7... | collective-permute-start | bytes 614408 | tf_op jit(solution)/shard_map/ppermute | solution.py:21
  56.4 5.6 %collective-permute-start = (f32[5,6,16,128]{3,2,1,0:T(8,128)S(1)}, f32[5,6,16,128]{3,2,1,0:T(8,128)S(1)}, u32[]{:S(2)}, u32[]{:S(2)}) collective-permute-start(f32[5,6,16,128]{3,2,1,0:T(8,128)S(1)} %get-tuple-element.997), channel_id=1, source_target_pairs={{8,0},{16,8},{24,16},{32,24},{40,32},{48,40},{56,48},{64,56},{72,6... | collective-permute-start | bytes 737288 | tf_op jit(solution)/shard_map/while/body/eval_jaxpr/ppermute | solution.py:33
  58.3 9.6 %collective-permute-start.1 = (f32[5,6,16,128]{3,2,1,0:T(8,128)S(1)}, f32[5,6,16,128]{3,2,1,0:T(8,128)S(1)}, u32[]{:S(2)}, u32[]{:S(2)}) collective-permute-start(f32[5,6,16,128]{3,2,1,0:T(8,128)S(1)} %get-tuple-element.996), channel_id=1, source_target_pairs={{0,8},{8,16},{16,24},{24,32},{32,40},{40,48},{48,56},{56,64},{64,7... | collective-permute-start | bytes 737288 | tf_op jit(solution)/shard_map/while/body/eval_jaxpr/ppermute | solution.py:33
  69.2 5.6 %collective-permute-start = (f32[5,6,16,128]{3,2,1,0:T(8,128)S(1)}, f32[5,6,16,128]{3,2,1,0:T(8,128)S(1)}, u32[]{:S(2)}, u32[]{:S(2)}) collective-permute-start(f32[5,6,16,128]{3,2,1,0:T(8,128)S(1)} %get-tuple-element.997), channel_id=1, source_target_pairs={{8,0},{16,8},{24,16},{32,24},{40,32},{48,40},{56,48},{64,56},{72,6... | collective-permute-start | bytes 737288 | tf_op jit(solution)/shard_map/while/body/eval_jaxpr/ppermute | solution.py:33
  71.1 9.6 %collective-permute-start.1 = (f32[5,6,16,128]{3,2,1,0:T(8,128)S(1)}, f32[5,6,16,128]{3,2,1,0:T(8,128)S(1)}, u32[]{:S(2)}, u32[]{:S(2)}) collective-permute-start(f32[5,6,16,128]{3,2,1,0:T(8,128)S(1)} %get-tuple-element.996), channel_id=1, source_target_pairs={{0,8},{8,16},{16,24},{24,32},{32,40},{40,48},{48,56},{56,64},{64,7... | collective-permute-start | bytes 737288 | tf_op jit(solution)/shard_map/while/body/eval_jaxpr/ppermute | solution.py:33
  82.0 5.6 %collective-permute-start = (f32[5,6,16,128]{3,2,1,0:T(8,128)S(1)}, f32[5,6,16,128]{3,2,1,0:T(8,128)S(1)}, u32[]{:S(2)}, u32[]{:S(2)}) collective-permute-start(f32[5,6,16,128]{3,2,1,0:T(8,128)S(1)} %get-tuple-element.997), channel_id=1, source_target_pairs={{8,0},{16,8},{24,16},{32,24},{40,32},{48,40},{56,48},{64,56},{72,6... | collective-permute-start | bytes 737288 | tf_op jit(solution)/shard_map/while/body/eval_jaxpr/ppermute | solution.py:33
  83.9 9.6 %collective-permute-start.1 = (f32[5,6,16,128]{3,2,1,0:T(8,128)S(1)}, f32[5,6,16,128]{3,2,1,0:T(8,128)S(1)}, u32[]{:S(2)}, u32[]{:S(2)}) collective-permute-start(f32[5,6,16,128]{3,2,1,0:T(8,128)S(1)} %get-tuple-element.996), channel_id=1, source_target_pairs={{0,8},{8,16},{16,24},{24,32},{32,40},{40,48},{48,56},{56,64},{64,7... | collective-permute-start | bytes 737288 | tf_op jit(solution)/shard_map/while/body/eval_jaxpr/ppermute | solution.py:33
  94.7 5.6 %collective-permute-start = (f32[5,6,16,128]{3,2,1,0:T(8,128)S(1)}, f32[5,6,16,128]{3,2,1,0:T(8,128)S(1)}, u32[]{:S(2)}, u32[]{:S(2)}) collective-permute-start(f32[5,6,16,128]{3,2,1,0:T(8,128)S(1)} %get-tuple-element.997), channel_id=1, source_target_pairs={{8,0},{16,8},{24,16},{32,24},{40,32},{48,40},{56,48},{64,56},{72,6... | collective-permute-start | bytes 737288 | tf_op jit(solution)/shard_map/while/body/eval_jaxpr/ppermute | solution.py:33
  96.7 9.6 %collective-permute-start.1 = (f32[5,6,16,128]{3,2,1,0:T(8,128)S(1)}, f32[5,6,16,128]{3,2,1,0:T(8,128)S(1)}, u32[]{:S(2)}, u32[]{:S(2)}) collective-permute-start(f32[5,6,16,128]{3,2,1,0:T(8,128)S(1)} %get-tuple-element.996), channel_id=1, source_target_pairs={{0,8},{8,16},{16,24},{24,32},{32,40},{40,48},{48,56},{56,64},{64,7... | collective-permute-start | bytes 737288 | tf_op jit(solution)/shard_map/while/body/eval_jaxpr/ppermute | solution.py:33
  107.5 5.6 %collective-permute-start = (f32[5,6,16,128]{3,2,1,0:T(8,128)S(1)}, f32[5,6,16,128]{3,2,1,0:T(8,128)S(1)}, u32[]{:S(2)}, u32[]{:S(2)}) collective-permute-start(f32[5,6,16,128]{3,2,1,0:T(8,128)S(1)} %get-tuple-element.997), channel_id=1, source_target_pairs={{8,0},{16,8},{24,16},{32,24},{40,32},{48,40},{56,48},{64,56},{72,6... | collective-permute-start | bytes 737288 | tf_op jit(solution)/shard_map/while/body/eval_jaxpr/ppermute | solution.py:33
  109.5 9.6 %collective-permute-start.1 = (f32[5,6,16,128]{3,2,1,0:T(8,128)S(1)}, f32[5,6,16,128]{3,2,1,0:T(8,128)S(1)}, u32[]{:S(2)}, u32[]{:S(2)}) collective-permute-start(f32[5,6,16,128]{3,2,1,0:T(8,128)S(1)} %get-tuple-element.996), channel_id=1, source_target_pairs={{0,8},{8,16},{16,24},{24,32},{32,40},{40,48},{48,56},{56,64},{64,7... | collective-permute-start | bytes 737288 | tf_op jit(solution)/shard_map/while/body/eval_jaxpr/ppermute | solution.py:33
  120.3 5.6 %collective-permute-start = (f32[5,6,16,128]{3,2,1,0:T(8,128)S(1)}, f32[5,6,16,128]{3,2,1,0:T(8,128)S(1)}, u32[]{:S(2)}, u32[]{:S(2)}) collective-permute-start(f32[5,6,16,128]{3,2,1,0:T(8,128)S(1)} %get-tuple-element.997), channel_id=1, source_target_pairs={{8,0},{16,8},{24,16},{32,24},{40,32},{48,40},{56,48},{64,56},{72,6... | collective-permute-start | bytes 737288 | tf_op jit(solution)/shard_map/while/body/eval_jaxpr/ppermute | solution.py:33
  122.3 9.6 %collective-permute-start.1 = (f32[5,6,16,128]{3,2,1,0:T(8,128)S(1)}, f32[5,6,16,128]{3,2,1,0:T(8,128)S(1)}, u32[]{:S(2)}, u32[]{:S(2)}) collective-permute-start(f32[5,6,16,128]{3,2,1,0:T(8,128)S(1)} %get-tuple-element.996), channel_id=1, source_target_pairs={{0,8},{8,16},{16,24},{24,32},{32,40},{40,48},{48,56},{56,64},{64,7... | collective-permute-start | bytes 737288 | tf_op jit(solution)/shard_map/while/body/eval_jaxpr/ppermute | solution.py:33
  133.1 5.6 %collective-permute-start = (f32[5,6,16,128]{3,2,1,0:T(8,128)S(1)}, f32[5,6,16,128]{3,2,1,0:T(8,128)S(1)}, u32[]{:S(2)}, u32[]{:S(2)}) collective-permute-start(f32[5,6,16,128]{3,2,1,0:T(8,128)S(1)} %get-tuple-element.997), channel_id=1, source_target_pairs={{8,0},{16,8},{24,16},{32,24},{40,32},{48,40},{56,48},{64,56},{72,6... | collective-permute-start | bytes 737288 | tf_op jit(solution)/shard_map/while/body/eval_jaxpr/ppermute | solution.py:33
  135.0 9.6 %collective-permute-start.1 = (f32[5,6,16,128]{3,2,1,0:T(8,128)S(1)}, f32[5,6,16,128]{3,2,1,0:T(8,128)S(1)}, u32[]{:S(2)}, u32[]{:S(2)}) collective-permute-start(f32[5,6,16,128]{3,2,1,0:T(8,128)S(1)} %get-tuple-element.996), channel_id=1, source_target_pairs={{0,8},{8,16},{16,24},{24,32},{32,40},{40,48},{48,56},{56,64},{64,7... | collective-permute-start | bytes 737288 | tf_op jit(solution)/shard_map/while/body/eval_jaxpr/ppermute | solution.py:33
  145.9 5.6 %collective-permute-start = (f32[5,6,16,128]{3,2,1,0:T(8,128)S(1)}, f32[5,6,16,128]{3,2,1,0:T(8,128)S(1)}, u32[]{:S(2)}, u32[]{:S(2)}) collective-permute-start(f32[5,6,16,128]{3,2,1,0:T(8,128)S(1)} %get-tuple-element.997), channel_id=1, source_target_pairs={{8,0},{16,8},{24,16},{32,24},{40,32},{48,40},{56,48},{64,56},{72,6... | collective-permute-start | bytes 737288 | tf_op jit(solution)/shard_map/while/body/eval_jaxpr/ppermute | solution.py:33
  147.8 9.6 %collective-permute-start.1 = (f32[5,6,16,128]{3,2,1,0:T(8,128)S(1)}, f32[5,6,16,128]{3,2,1,0:T(8,128)S(1)}, u32[]{:S(2)}, u32[]{:S(2)}) collective-permute-start(f32[5,6,16,128]{3,2,1,0:T(8,128)S(1)} %get-tuple-element.996), channel_id=1, source_target_pairs={{0,8},{8,16},{16,24},{24,32},{32,40},{40,48},{48,56},{56,64},{64,7... | collective-permute-start | bytes 737288 | tf_op jit(solution)/shard_map/while/body/eval_jaxpr/ppermute | solution.py:33
  158.7 5.6 %collective-permute-start = (f32[5,6,16,128]{3,2,1,0:T(8,128)S(1)}, f32[5,6,16,128]{3,2,1,0:T(8,128)S(1)}, u32[]{:S(2)}, u32[]{:S(2)}) collective-permute-start(f32[5,6,16,128]{3,2,1,0:T(8,128)S(1)} %get-tuple-element.997), channel_id=1, source_target_pairs={{8,0},{16,8},{24,16},{32,24},{40,32},{48,40},{56,48},{64,56},{72,6... | collective-permute-start | bytes 737288 | tf_op jit(solution)/shard_map/while/body/eval_jaxpr/ppermute | solution.py:33
  160.6 9.6 %collective-permute-start.1 = (f32[5,6,16,128]{3,2,1,0:T(8,128)S(1)}, f32[5,6,16,128]{3,2,1,0:T(8,128)S(1)}, u32[]{:S(2)}, u32[]{:S(2)}) collective-permute-start(f32[5,6,16,128]{3,2,1,0:T(8,128)S(1)} %get-tuple-element.996), channel_id=1, source_target_pairs={{0,8},{8,16},{16,24},{24,32},{32,40},{40,48},{48,56},{56,64},{64,7... | collective-permute-start | bytes 737288 | tf_op jit(solution)/shard_map/while/body/eval_jaxpr/ppermute | solution.py:33
  171.5 5.6 %collective-permute-start = (f32[5,6,16,128]{3,2,1,0:T(8,128)S(1)}, f32[5,6,16,128]{3,2,1,0:T(8,128)S(1)}, u32[]{:S(2)}, u32[]{:S(2)}) collective-permute-start(f32[5,6,16,128]{3,2,1,0:T(8,128)S(1)} %get-tuple-element.997), channel_id=1, source_target_pairs={{8,0},{16,8},{24,16},{32,24},{40,32},{48,40},{56,48},{64,56},{72,6... | collective-permute-start | bytes 737288 | tf_op jit(solution)/shard_map/while/body/eval_jaxpr/ppermute | solution.py:33
  173.4 9.6 %collective-permute-start.1 = (f32[5,6,16,128]{3,2,1,0:T(8,128)S(1)}, f32[5,6,16,128]{3,2,1,0:T(8,128)S(1)}, u32[]{:S(2)}, u32[]{:S(2)}) collective-permute-start(f32[5,6,16,128]{3,2,1,0:T(8,128)S(1)} %get-tuple-element.996), channel_id=1, source_target_pairs={{0,8},{8,16},{16,24},{24,32},{32,40},{40,48},{48,56},{56,64},{64,7... | collective-permute-start | bytes 737288 | tf_op jit(solution)/shard_map/while/body/eval_jaxpr/ppermute | solution.py:33
  184.3 5.6 %collective-permute-start = (f32[5,6,16,128]{3,2,1,0:T(8,128)S(1)}, f32[5,6,16,128]{3,2,1,0:T(8,128)S(1)}, u32[]{:S(2)}, u32[]{:S(2)}) collective-permute-start(f32[5,6,16,128]{3,2,1,0:T(8,128)S(1)} %get-tuple-element.997), channel_id=1, source_target_pairs={{8,0},{16,8},{24,16},{32,24},{40,32},{48,40},{56,48},{64,56},{72,6... | collective-permute-start | bytes 737288 | tf_op jit(solution)/shard_map/while/body/eval_jaxpr/ppermute | solution.py:33
  186.2 9.6 %collective-permute-start.1 = (f32[5,6,16,128]{3,2,1,0:T(8,128)S(1)}, f32[5,6,16,128]{3,2,1,0:T(8,128)S(1)}, u32[]{:S(2)}, u32[]{:S(2)}) collective-permute-start(f32[5,6,16,128]{3,2,1,0:T(8,128)S(1)} %get-tuple-element.996), channel_id=1, source_target_pairs={{0,8},{8,16},{16,24},{24,32},{32,40},{40,48},{48,56},{56,64},{64,7... | collective-permute-start | bytes 737288 | tf_op jit(solution)/shard_map/while/body/eval_jaxpr/ppermute | solution.py:33
  197.1 5.6 %collective-permute-start = (f32[5,6,16,128]{3,2,1,0:T(8,128)S(1)}, f32[5,6,16,128]{3,2,1,0:T(8,128)S(1)}, u32[]{:S(2)}, u32[]{:S(2)}) collective-permute-start(f32[5,6,16,128]{3,2,1,0:T(8,128)S(1)} %get-tuple-element.997), channel_id=1, source_target_pairs={{8,0},{16,8},{24,16},{32,24},{40,32},{48,40},{56,48},{64,56},{72,6... | collective-permute-start | bytes 737288 | tf_op jit(solution)/shard_map/while/body/eval_jaxpr/ppermute | solution.py:33
  199.0 9.6 %collective-permute-start.1 = (f32[5,6,16,128]{3,2,1,0:T(8,128)S(1)}, f32[5,6,16,128]{3,2,1,0:T(8,128)S(1)}, u32[]{:S(2)}, u32[]{:S(2)}) collective-permute-start(f32[5,6,16,128]{3,2,1,0:T(8,128)S(1)} %get-tuple-element.996), channel_id=1, source_target_pairs={{0,8},{8,16},{16,24},{24,32},{32,40},{40,48},{48,56},{56,64},{64,7... | collective-permute-start | bytes 737288 | tf_op jit(solution)/shard_map/while/body/eval_jaxpr/ppermute | solution.py:33
  209.8 5.6 %collective-permute-start = (f32[5,6,16,128]{3,2,1,0:T(8,128)S(1)}, f32[5,6,16,128]{3,2,1,0:T(8,128)S(1)}, u32[]{:S(2)}, u32[]{:S(2)}) collective-permute-start(f32[5,6,16,128]{3,2,1,0:T(8,128)S(1)} %get-tuple-element.997), channel_id=1, source_target_pairs={{8,0},{16,8},{24,16},{32,24},{40,32},{48,40},{56,48},{64,56},{72,6... | collective-permute-start | bytes 737288 | tf_op jit(solution)/shard_map/while/body/eval_jaxpr/ppermute | solution.py:33
  211.8 9.6 %collective-permute-start.1 = (f32[5,6,16,128]{3,2,1,0:T(8,128)S(1)}, f32[5,6,16,128]{3,2,1,0:T(8,128)S(1)}, u32[]{:S(2)}, u32[]{:S(2)}) collective-permute-start(f32[5,6,16,128]{3,2,1,0:T(8,128)S(1)} %get-tuple-element.996), channel_id=1, source_target_pairs={{0,8},{8,16},{16,24},{24,32},{32,40},{40,48},{48,56},{56,64},{64,7... | collective-permute-start | bytes 737288 | tf_op jit(solution)/shard_map/while/body/eval_jaxpr/ppermute | solution.py:33
  224.6 9.6 %collective-permute-start.1 = (f32[5,6,16,128]{3,2,1,0:T(8,128)S(1)}, f32[5,6,16,128]{3,2,1,0:T(8,128)S(1)}, u32[]{:S(2)}, u32[]{:S(2)}) collective-permute-start(f32[5,6,16,128]{3,2,1,0:T(8,128)S(1)} %get-tuple-element.996), channel_id=1, source_target_pairs={{0,8},{8,16},{16,24},{24,32},{32,40},{40,48},{48,56},{56,64},{64,7... | collective-permute-start | bytes 737288 | tf_op jit(solution)/shard_map/while/body/eval_jaxpr/ppermute | solution.py:33
  237.4 9.6 %collective-permute-start.1 = (f32[5,6,16,128]{3,2,1,0:T(8,128)S(1)}, f32[5,6,16,128]{3,2,1,0:T(8,128)S(1)}, u32[]{:S(2)}, u32[]{:S(2)}) collective-permute-start(f32[5,6,16,128]{3,2,1,0:T(8,128)S(1)} %get-tuple-element.996), channel_id=1, source_target_pairs={{0,8},{8,16},{16,24},{24,32},{32,40},{40,48},{48,56},{56,64},{64,7... | collective-permute-start | bytes 737288 | tf_op jit(solution)/shard_map/while/body/eval_jaxpr/ppermute | solution.py:33
  250.1 9.6 %collective-permute-start.1 = (f32[5,6,16,128]{3,2,1,0:T(8,128)S(1)}, f32[5,6,16,128]{3,2,1,0:T(8,128)S(1)}, u32[]{:S(2)}, u32[]{:S(2)}) collective-permute-start(f32[5,6,16,128]{3,2,1,0:T(8,128)S(1)} %get-tuple-element.996), channel_id=1, source_target_pairs={{0,8},{8,16},{16,24},{24,32},{32,40},{40,48},{48,56},{56,64},{64,7... | collective-permute-start | bytes 737288 | tf_op jit(solution)/shard_map/while/body/eval_jaxpr/ppermute | solution.py:33
  262.9 9.6 %collective-permute-start.1 = (f32[5,6,16,128]{3,2,1,0:T(8,128)S(1)}, f32[5,6,16,128]{3,2,1,0:T(8,128)S(1)}, u32[]{:S(2)}, u32[]{:S(2)}) collective-permute-start(f32[5,6,16,128]{3,2,1,0:T(8,128)S(1)} %get-tuple-element.996), channel_id=1, source_target_pairs={{0,8},{8,16},{16,24},{24,32},{32,40},{40,48},{48,56},{56,64},{64,7... | collective-permute-start | bytes 737288 | tf_op jit(solution)/shard_map/while/body/eval_jaxpr/ppermute | solution.py:33
  275.7 9.6 %collective-permute-start.1 = (f32[5,6,16,128]{3,2,1,0:T(8,128)S(1)}, f32[5,6,16,128]{3,2,1,0:T(8,128)S(1)}, u32[]{:S(2)}, u32[]{:S(2)}) collective-permute-start(f32[5,6,16,128]{3,2,1,0:T(8,128)S(1)} %get-tuple-element.996), channel_id=1, source_target_pairs={{0,8},{8,16},{16,24},{24,32},{32,40},{40,48},{48,56},{56,64},{64,7... | collective-permute-start | bytes 737288 | tf_op jit(solution)/shard_map/while/body/eval_jaxpr/ppermute | solution.py:33
  288.5 9.6 %collective-permute-start.1 = (f32[5,6,16,128]{3,2,1,0:T(8,128)S(1)}, f32[5,6,16,128]{3,2,1,0:T(8,128)S(1)}, u32[]{:S(2)}, u32[]{:S(2)}) collective-permute-start(f32[5,6,16,128]{3,2,1,0:T(8,128)S(1)} %get-tuple-element.996), channel_id=1, source_target_pairs={{0,8},{8,16},{16,24},{24,32},{32,40},{40,48},{48,56},{56,64},{64,7... | collective-permute-start | bytes 737288 | tf_op jit(solution)/shard_map/while/body/eval_jaxpr/ppermute | solution.py:33
  301.3 9.6 %collective-permute-start.1 = (f32[5,6,16,128]{3,2,1,0:T(8,128)S(1)}, f32[5,6,16,128]{3,2,1,0:T(8,128)S(1)}, u32[]{:S(2)}, u32[]{:S(2)}) collective-permute-start(f32[5,6,16,128]{3,2,1,0:T(8,128)S(1)} %get-tuple-element.996), channel_id=1, source_target_pairs={{0,8},{8,16},{16,24},{24,32},{32,40},{40,48},{48,56},{56,64},{64,7... | collective-permute-start | bytes 737288 | tf_op jit(solution)/shard_map/while/body/eval_jaxpr/ppermute | solution.py:33
  314.1 9.6 %collective-permute-start.1 = (f32[5,6,16,128]{3,2,1,0:T(8,128)S(1)}, f32[5,6,16,128]{3,2,1,0:T(8,128)S(1)}, u32[]{:S(2)}, u32[]{:S(2)}) collective-permute-start(f32[5,6,16,128]{3,2,1,0:T(8,128)S(1)} %get-tuple-element.996), channel_id=1, source_target_pairs={{0,8},{8,16},{16,24},{24,32},{32,40},{40,48},{48,56},{56,64},{64,7... | collective-permute-start | bytes 737288 | tf_op jit(solution)/shard_map/while/body/eval_jaxpr/ppermute | solution.py:33
  326.9 9.6 %collective-permute-start.1 = (f32[5,6,16,128]{3,2,1,0:T(8,128)S(1)}, f32[5,6,16,128]{3,2,1,0:T(8,128)S(1)}, u32[]{:S(2)}, u32[]{:S(2)}) collective-permute-start(f32[5,6,16,128]{3,2,1,0:T(8,128)S(1)} %get-tuple-element.996), channel_id=1, source_target_pairs={{0,8},{8,16},{16,24},{24,32},{32,40},{40,48},{48,56},{56,64},{64,7... | collective-permute-start | bytes 737288 | tf_op jit(solution)/shard_map/while/body/eval_jaxpr/ppermute | solution.py:33
  339.7 9.6 %collective-permute-start.1 = (f32[5,6,16,128]{3,2,1,0:T(8,128)S(1)}, f32[5,6,16,128]{3,2,1,0:T(8,128)S(1)}, u32[]{:S(2)}, u32[]{:S(2)}) collective-permute-start(f32[5,6,16,128]{3,2,1,0:T(8,128)S(1)} %get-tuple-element.996), channel_id=1, source_target_pairs={{0,8},{8,16},{16,24},{24,32},{32,40},{40,48},{48,56},{56,64},{64,7... | collective-permute-start | bytes 737288 | tf_op jit(solution)/shard_map/while/body/eval_jaxpr/ppermute | solution.py:33
  352.5 9.6 %collective-permute-start.1 = (f32[5,6,16,128]{3,2,1,0:T(8,128)S(1)}, f32[5,6,16,128]{3,2,1,0:T(8,128)S(1)}, u32[]{:S(2)}, u32[]{:S(2)}) collective-permute-start(f32[5,6,16,128]{3,2,1,0:T(8,128)S(1)} %get-tuple-element.996), channel_id=1, source_target_pairs={{0,8},{8,16},{16,24},{24,32},{32,40},{40,48},{48,56},{56,64},{64,7... | collective-permute-start | bytes 737288 | tf_op jit(solution)/shard_map/while/body/eval_jaxpr/ppermute | solution.py:33
  365.2 9.6 %collective-permute-start.1 = (f32[5,6,16,128]{3,2,1,0:T(8,128)S(1)}, f32[5,6,16,128]{3,2,1,0:T(8,128)S(1)}, u32[]{:S(2)}, u32[]{:S(2)}) collective-permute-start(f32[5,6,16,128]{3,2,1,0:T(8,128)S(1)} %get-tuple-element.996), channel_id=1, source_target_pairs={{0,8},{8,16},{16,24},{24,32},{32,40},{40,48},{48,56},{56,64},{64,7... | collective-permute-start | bytes 737288 | tf_op jit(solution)/shard_map/while/body/eval_jaxpr/ppermute | solution.py:33
  378.0 9.6 %collective-permute-start.1 = (f32[5,6,16,128]{3,2,1,0:T(8,128)S(1)}, f32[5,6,16,128]{3,2,1,0:T(8,128)S(1)}, u32[]{:S(2)}, u32[]{:S(2)}) collective-permute-start(f32[5,6,16,128]{3,2,1,0:T(8,128)S(1)} %get-tuple-element.996), channel_id=1, source_target_pairs={{0,8},{8,16},{16,24},{24,32},{32,40},{40,48},{48,56},{56,64},{64,7... | collective-permute-start | bytes 737288 | tf_op jit(solution)/shard_map/while/body/eval_jaxpr/ppermute | solution.py:33
  390.8 9.6 %collective-permute-start.1 = (f32[5,6,16,128]{3,2,1,0:T(8,128)S(1)}, f32[5,6,16,128]{3,2,1,0:T(8,128)S(1)}, u32[]{:S(2)}, u32[]{:S(2)}) collective-permute-start(f32[5,6,16,128]{3,2,1,0:T(8,128)S(1)} %get-tuple-element.996), channel_id=1, source_target_pairs={{0,8},{8,16},{16,24},{24,32},{32,40},{40,48},{48,56},{56,64},{64,7... | collective-permute-start | bytes 737288 | tf_op jit(solution)/shard_map/while/body/eval_jaxpr/ppermute | solution.py:33
  403.6 9.6 %collective-permute-start.1 = (f32[5,6,16,128]{3,2,1,0:T(8,128)S(1)}, f32[5,6,16,128]{3,2,1,0:T(8,128)S(1)}, u32[]{:S(2)}, u32[]{:S(2)}) collective-permute-start(f32[5,6,16,128]{3,2,1,0:T(8,128)S(1)} %get-tuple-element.996), channel_id=1, source_target_pairs={{0,8},{8,16},{16,24},{24,32},{32,40},{40,48},{48,56},{56,64},{64,7... | collective-permute-start | bytes 737288 | tf_op jit(solution)/shard_map/while/body/eval_jaxpr/ppermute | solution.py:33
  416.4 9.6 %collective-permute-start.1 = (f32[5,6,16,128]{3,2,1,0:T(8,128)S(1)}, f32[5,6,16,128]{3,2,1,0:T(8,128)S(1)}, u32[]{:S(2)}, u32[]{:S(2)}) collective-permute-start(f32[5,6,16,128]{3,2,1,0:T(8,128)S(1)} %get-tuple-element.996), channel_id=1, source_target_pairs={{0,8},{8,16},{16,24},{24,32},{32,40},{40,48},{48,56},{56,64},{64,7... | collective-permute-start | bytes 737288 | tf_op jit(solution)/shard_map/while/body/eval_jaxpr/ppermute | solution.py:33
  429.2 9.6 %collective-permute-start.1 = (f32[5,6,16,128]{3,2,1,0:T(8,128)S(1)}, f32[5,6,16,128]{3,2,1,0:T(8,128)S(1)}, u32[]{:S(2)}, u32[]{:S(2)}) collective-permute-start(f32[5,6,16,128]{3,2,1,0:T(8,128)S(1)} %get-tuple-element.996), channel_id=1, source_target_pairs={{0,8},{8,16},{16,24},{24,32},{32,40},{40,48},{48,56},{56,64},{64,7... | collective-permute-start | bytes 737288 | tf_op jit(solution)/shard_map/while/body/eval_jaxpr/ppermute | solution.py:33
  442.0 9.6 %collective-permute-start.1 = (f32[5,6,16,128]{3,2,1,0:T(8,128)S(1)}, f32[5,6,16,128]{3,2,1,0:T(8,128)S(1)}, u32[]{:S(2)}, u32[]{:S(2)}) collective-permute-start(f32[5,6,16,128]{3,2,1,0:T(8,128)S(1)} %get-tuple-element.996), channel_id=1, source_target_pairs={{0,8},{8,16},{16,24},{24,32},{32,40},{40,48},{48,56},{56,64},{64,7... | collective-permute-start | bytes 737288 | tf_op jit(solution)/shard_map/while/body/eval_jaxpr/ppermute | solution.py:33
  (86 other events, 184.7 us)
where the time goes:
time: 467 us; the launch traced here: 461 us
  waiting for transfers between devices  201 us (43%)
  starting transfers between devices  147 us (31%)
  other arithmetic  65.9 us (14%)
  local copies, waits for them, and re-layouts  27.5 us (6%)
  loops' own time  18.5 us (4%)
    ppermute x62, waiting for transfers between devices, shifted(): return lax.ppermute(block, axis, route)  195 us
    ppermute x62, starting transfers between devices, shifted(): return lax.ppermute(block, axis, route)  134 us
    reduce_sum x234, other arithmetic, mat_mul(): return jnp.sum(left[:, :, None] * right[None], axis=1)  19.8 us
    another operation x1, loops' own time, on_device(): lax.fori_loop(0, lax.axis_size('stream') - 1, relay, begin)  17.5 us
  transfers between devices with their start and end apart: 66, of which 63 were waited for; matrix products, arithmetic and copies ran while one was open for 4% of the time, Pallas kernels for 0%

commit v1 on v0

v1 whole, which is shorter than its diff:
```python
import jax
import jax.numpy as jnp
from jax import lax
from jax.experimental import pallas as pl
from jax.experimental.pallas import tpu as pltpu
from jax.sharding import PartitionSpec as P

N = 32
R = 16
HALF = 64
MESH = pl.DeviceIdType.MESH


def roll_lanes(x):
    return pltpu.roll(x, HALF, axis=x.ndim - 1)


def roll_rows(x, by):
    return pltpu.roll(x, by % 8, axis=x.ndim - 2)


def swap_halves(a, b):
    low = lax.broadcasted_iota(jnp.int32, a.shape, a.ndim - 1) < HALF
    return jnp.where(low, a, roll_lanes(b)), jnp.where(low, roll_lanes(a), b)


def place(shape):
    q = lax.broadcasted_iota(jnp.int32, shape, len(shape) - 2)
    b = lax.broadcasted_iota(jnp.int32, shape, len(shape) - 1) >= HALF
    return q, b


def previous(x, by):
    q, b = place(x.shape)
    if by == 1:
        moved = roll_lanes(jnp.where(b, roll_rows(x, 1), x))
        return jnp.where((q == 0) & ~b, 0.0, moved)
    return jnp.where(q < by // 2, 0.0, roll_rows(x, by // 2))


def following(x, by):
    q, b = place(x.shape)
    if by == 1:
        moved = roll_lanes(jnp.where(b, x, roll_rows(x, -1)))
        return jnp.where((q == 7) & b, 0.0, moved)
    return jnp.where(q >= 8 - by // 2, 0.0, roll_rows(x, -(by // 2)))


def jacobian_rows(u, v, w, h, k):
    return [
        [None, 1.0, None, None, None],
        [0.4 * k - u * u, 1.6 * u, -0.4 * v, -0.4 * w, 0.4],
        [-u * v, v, u, None, None],
        [-u * w, w, None, u, None],
        [u * (0.4 * k - h), h - 0.4 * u * u, -0.4 * u * v, -0.4 * u * w, 1.4 * u],
    ]


def jacobian_times(prm, m):
    u, v, w, h, k = prm
    t = m[1] - u * m[0]
    p = 0.4 * (k * m[0] - u * m[1] - v * m[2] - w * m[3] + m[4])
    return [
        m[1],
        p + u * (m[1] + t),
        v * t + u * m[2],
        w * t + u * m[3],
        u * (p + m[4]) + h * t,
    ]


def row_times_jacobian(g, prm, shift):
    u, v, w, h, k = prm
    e = g[0]
    for value, factor in ((g[1], u), (g[2], v), (g[3], w), (g[4], h)):
        if value is not None:
            e = value * factor if e is None else e + value * factor
    p = g[1] if g[4] is None else g[1] + u * g[4]
    p = 0.4 * p
    s = u + shift

    def part(index, other):
        return other if g[index] is None else s * g[index] + other

    return [
        part(0, k * p - u * e),
        part(1, e - u * p),
        part(2, -(v * p)),
        part(3, -(w * p)),
        part(4, p),
    ]


def scaled(rows, shift, factor):
    out = []
    for r in range(5):
        row = []
        for c in range(5):
            value = rows[r][c]
            if r == c:
                value = shift if value is None else value + shift
            row.append(None if value is None else value * factor)
        out.append(row)
    return out


def plus(a, b):
    if a is None:
        return b
    return a if b is None else a + b


def factor_rows(rows):
    rows = list(rows)
    recip = []
    for p in range(5):
        rec = 1.0 / rows[p][p]
        recip.append(rec)
        for r in range(p + 1, 5):
            weight = rows[r][p] * rec
            tail = rows[r][p + 1 :] - weight[None] * rows[p][p + 1 :] if p < 4 else None
            parts = [rows[r][:p], weight[None], tail] if p else [weight[None], tail]
            rows[r] = jnp.concatenate(parts, axis=0)
    return rows, recip


def solve_rows(lu, recip, right):
    x = list(right)
    for p in range(5):
        for r in range(p + 1, 5):
            x[r] = x[r] - lu[r][p] * x[p]
    for p in range(4, -1, -1):
        x[p] = x[p] * recip[p]
        for r in range(p):
            x[r] = x[r] - lu[r][p] * x[p]
    return x


def normalise(d_ref, x_ref, s):
    lu, recip = factor_rows([d_ref[s, r] for r in range(5)])
    x = solve_rows(lu, recip, [x_ref[s, r] for r in range(5)])
    for r in range(5):
        pieces = [lu[r][:r], recip[r][None], lu[r][r + 1 :]]
        d_ref[s, r] = jnp.concatenate([p for p in pieces if p.shape[0]], axis=0)
        x_ref[s, r] = x[r]


def solve_with(d_ref, s, right):
    lu = [d_ref[s, r] for r in range(5)]
    return solve_rows(lu, [lu[r][r] for r in range(5)], right)


def row_times(row, others):
    total = row[0] * others[0]
    for m in range(1, 5):
        total = total + row[m] * others[m]
    return total


def combine(own, diagonal, before, after, d_ref, x_ref, s):
    for r in range(5):
        left = row_times(own[r][:5], before)
        right = row_times(own[r][5:], after)
        d_ref[s, r] = diagonal[r] - left[5:] - right[:5]
        x_ref[s, r] = jnp.concatenate([-left[:5], -right[5:]], axis=0)


def subtract(own, r, before, after):
    return r - row_times(own[:5], before) - row_times(own[5:], after)


def kernel(
    state_ref, visc_ref, resid_ref, out_ref,
    st, vis, res, ss, gg, send_m, recv_m, send_r, recv_r, send_x, recv_x,
    prm, d1, x1, d2, x2, dp, xp, rr, xx,
    in_sem, halo_send, halo_recv, a2a_send, a2a_recv, own_sem,
):
    me = lax.axis_index("stream")
    z = lax.axis_index("normal")
    z_count = lax.axis_size("normal")
    z_up = lax.rem(z + 1, z_count)
    z_down = lax.rem(z + z_count - 1, z_count)

    loads = [
        pltpu.make_async_copy(state_ref, st.at[:, :, pl.ds(8, 16), :], in_sem.at[0]),
        pltpu.make_async_copy(visc_ref, vis, in_sem.at[1]),
        pltpu.make_async_copy(resid_ref, res, in_sem.at[2]),
    ]
    for load in loads:
        load.start()

    barrier = pltpu.get_barrier_semaphore()

    def greet(k, carry):
        pl.semaphore_signal(barrier, inc=1, device_id={"stream": lax.rem(me + k, N)}, device_id_type=MESH)
        return carry

    lax.fori_loop(1, N, greet, 0)
    for other in (z_up, z_down):
        pl.semaphore_signal(barrier, inc=1, device_id={"normal": other}, device_id_type=MESH)

    def message(buf, t):
        return buf.at[pl.ds(pl.multiple_of(t * R, R), R)]

    def exchange(send, recv, which):
        def go(k, carry):
            t = lax.rem(me + k, N)
            pltpu.make_async_remote_copy(
                src_ref=message(send, t), dst_ref=message(recv, me),
                send_sem=a2a_send.at[which], recv_sem=a2a_recv.at[which],
                device_id={"stream": t}, device_id_type=MESH,
            ).start()
            return carry

        lax.fori_loop(1, N, go, 0)
        pltpu.make_async_copy(message(send, me), message(recv, me), own_sem.at[which]).start()

    def all_of(send, recv, which):
        return pltpu.make_async_remote_copy(
            src_ref=send.at[pl.ds(0, (N - 1) * R)], dst_ref=recv.at[pl.ds(0, (N - 1) * R)],
            send_sem=a2a_send.at[which], recv_sem=a2a_recv.at[which],
            device_id={"stream": lax.rem(me + 1, N)}, device_id_type=MESH,
        )

    def arrived(send, recv, which):
        all_of(send, recv, which).wait_recv()
        pltpu.make_async_copy(message(send, me), message(recv, me), own_sem.at[which]).wait()

    def put(send, row, a, b):
        for h, rows in enumerate(swap_halves(a, b)):
            send[pl.ds(h * R + row, 16, stride=2 * R), :] = rows

    loads[0].wait()
    loads[1].wait()
    for c in range(2):
        pair = []
        for cell in (c, c + 2):
            rho, m1, m2, m3, energy = (st[p, cell, pl.ds(8, 16), :] for p in range(5))
            inverse = 1.0 / rho
            u, v, w = m1 * inverse, m2 * inverse, m3 * inverse
            h = 1.4 * energy * inverse - 0.2 * (u * u + v * v + w * w)
            pair.append((u, v, w, h, vis[cell]))
        for p in range(5):
            put(send_m, 2 * p + c, pair[0][p], pair[1][p])

    pl.semaphore_wait(barrier, N + 1)
    halos = [
        pltpu.make_async_remote_copy(
            src_ref=st.at[:, :, pl.ds(16, 8), :], dst_ref=st.at[:, :, pl.ds(0, 8), :],
            send_sem=halo_send.at[0], recv_sem=halo_recv.at[0],
            device_id={"normal": z_up}, device_id_type=MESH,
        ),
        pltpu.make_async_remote_copy(
            src_ref=st.at[:, :, pl.ds(8, 8), :], dst_ref=st.at[:, :, pl.ds(24, 8), :],
            send_sem=halo_send.at[1], recv_sem=halo_recv.at[1],
            device_id={"normal": z_down}, device_id_type=MESH,
        ),
    ]
    for halo in halos:
        halo.start()
    exchange(send_m, recv_m, 0)

    loads[2].wait()
    for halo in halos:
        halo.wait_recv()
    row = lax.broadcasted_iota(jnp.int32, (32, 128), 0)
    valid = (row >= jnp.where(z == 0, 8, 0)) & (row < jnp.where(z == z_count - 1, 24, 32))

    def right_side(c, carry):
        pair = []
        for cell in (c, c + 2):
            q = [st[p, cell] for p in range(5)]
            rho, m1, m2, m3, energy = q
            inverse = 1.0 / rho
            pressure = 0.4 * (energy - 0.5 * (m1 * m1 + m2 * m2 + m3 * m3) * inverse)
            v = m2 * inverse
            flux = [m2, m1 * v, m2 * v + pressure, m3 * v, (energy + pressure) * v]
            sigma = vis[cell]
            values = []
            for p in range(5):
                ss[p] = jnp.where(valid, q[p], 0.0)
                gg[p] = jnp.where(valid, flux[p], 0.0)
                s = {d: ss[p, pl.ds(8 + d, 16), :] for d in (-2, -1, 0, 1, 2)}
                values.append(
                    res[p, cell]
                    - 40.0 * (gg[p, pl.ds(9, 16), :] - gg[p, pl.ds(7, 16), :])
                    + sigma * (s[1] - 2.0 * s[0] + s[-1])
                    - 8.0 * (s[2] - 4.0 * s[1] + 6.0 * s[0] - 4.0 * s[-1] + s[-2])
                )
            pair.append(values)
        for p in range(5):
            put(send_r, 2 * p + c, pair[0][p], pair[1][p])
        return carry

    for c in range(2):
        right_side(c, 0)
    exchange(send_r, recv_r, 1)

    def get(recv, row, e):
        return swap_halves(*(recv[pl.ds((2 * b + e) * R + row, 8, stride=4 * R), :] for b in range(2)))

    arrived(send_m, recv_m, 0)
    for e in range(2):
        for c in range(2):
            both = [get(recv_m, 2 * p + c, e) for p in range(5)]
            for side in range(2):
                u, v, w, h, sigma = (both[p][side] for p in range(5))
                k = 0.5 * (u * u + v * v + w * w)
                cell = 4 * e + c + 2 * side
                values = (u, v, w, h, k, sigma, 1.0 / (1.0 + 2.0 * sigma))
                for p in range(7):
                    prm[p, cell + 2] = values[p]
                    if cell >= 6:
                        prm[p, cell - 6] = previous(values[p], 1)
                    if cell == 0:
                        prm[p, 10] = following(values[p], 1)

    def gas(place_):
        return tuple(prm[p, place_] for p in range(5))

    def level_1(i, carry):
        at = 2 * i + 2
        sigma, before, after = prm[5, at], prm[5, at - 1], prm[5, at + 1]
        left = scaled(jacobian_rows(*gas(at - 1)), sigma, prm[6, at - 1])
        right = scaled(jacobian_rows(*gas(at + 1)), -sigma, prm[6, at + 1])
        here, far_left, far_right = gas(at), gas(at - 2), gas(at + 2)
        for r in range(5):
            both = [plus(left[r][c], right[r][c]) for c in range(5)]
            own = row_times_jacobian(both, here, 0.0)
            for c in range(5):
                if left[r][c] is not None:
                    own[c] = own[c] + (after * right[r][c] - before * left[r][c])
            own[r] = own[r] + (1.0 + 2.0 * sigma)
            lower = row_times_jacobian(left[r], far_left, before)
            upper = row_times_jacobian(right[r], far_right, -after)
            for c in range(5):
                d1[i + 1, r, c] = own[c]
                x1[i + 1, r, c] = -lower[c]
                x1[i + 1, r, 5 + c] = -upper[c]
        return carry

    lax.fori_loop(0, 4, level_1, 0)

    def level_2_normalise(i, carry):
        normalise(d1, x1, 2 * i + 2)
        return carry

    lax.fori_loop(0, 2, level_2_normalise, 0)
    for r in range(5):
        x1[0, r] = previous(x1[4, r], 1)

    def rows_of(ref, s):
        return [ref[s, r] for r in range(5)]

    def level_2_combine(i, carry):
        s = 2 * i + 1
        combine(rows_of(x1, s), rows_of(d1, s), rows_of(x1, s - 1), rows_of(x1, s + 1), d2, x2, i)
        return carry

    lax.fori_loop(0, 2, level_2_combine, 0)

    normalise(d2, x2, 1)
    combine(
        rows_of(x2, 0), rows_of(d2, 0), [previous(x2[1, r], 1) for r in range(5)], rows_of(x2, 1), dp, xp, 0
    )

    unit = jnp.ones((8, 128), jnp.float32)
    nought = jnp.zeros((8, 128), jnp.float32)
    identity = [jnp.stack([unit if r == c else nought for c in range(5)]) for r in range(5)]
    for step in range(3):
        normalise(dp, xp, step)
        own = rows_of(xp, step)
        combine(
            own, identity, [previous(x, 2**step) for x in own], [following(x, 2**step) for x in own],
            dp, xp, step + 1,
        )
    lu, recip = factor_rows(rows_of(dp, 3))
    q, _ = place((5, 8, 128))
    other = [jnp.where(q < 4, xp[3, r, pl.ds(5, 5)], xp[3, r, pl.ds(0, 5)]) for r in range(5)]
    other = solve_rows(lu, recip, other)
    partner = [roll_rows(x, 4) for x in other]
    last, last_recip = factor_rows([identity[r] - row_times(other[r], partner) for r in range(5)])

    arrived(send_r, recv_r, 1)
    for e in range(2):
        for c in range(2):
            for p in range(5):
                a, b = get(recv_r, 2 * p + c, e)
                rr[4 * e + c, p] = a
                rr[4 * e + c + 2, p] = b

    def column(ref, i):
        return [ref[i, p] for p in range(5)]

    odd = {}
    for i in (1, 3, 5, 7):
        y = [prm[6, i + 2] * value for value in column(rr, i)]
        odd[i] = y, jacobian_times(gas(i + 2), y)
    odd[-1] = tuple([previous(value, 1) for value in part] for part in odd[7])
    even = {}
    for i in (0, 2, 4, 6):
        sigma = prm[5, i + 2]
        (y0, f0), (y1, f1) = odd[i - 1], odd[i + 1]
        even[i] = [rr[i, p] + sigma * (y0[p] + y1[p]) + (f0[p] - f1[p]) for p in range(5)]
    y = {i: solve_with(d1, i // 2 + 1, even[i]) for i in (2, 6)}
    y[-2] = [previous(value, 1) for value in y[6]]
    four = {}
    for i in (0, 4):
        four[i] = [subtract(x1[i // 2 + 1, r], even[i][r], y[i - 2], y[i + 2]) for r in range(5)]
    y[4] = solve_with(d2, 1, four[4])
    before = [previous(value, 1) for value in y[4]]
    b = [subtract(x2[0, r], four[0][r], before, y[4]) for r in range(5)]
    for step in range(3):
        b = solve_with(dp, step, b)
        before = [previous(value, 2**step) for value in b]
        after = [following(value, 2**step) for value in b]
        b = [subtract(xp[step, r], b[r], before, after) for r in range(5)]
    b = solve_rows(lu, recip, b)
    paired = [roll_rows(value, 4) for value in b]
    b = [b[r] - row_times(other[r], paired) for r in range(5)]
    x = {0: solve_rows(last, last_recip, b)}
    x[8] = [following(value, 1) for value in x[0]]
    x[4] = [subtract(x2[1, r], y[4][r], x[0], x[8]) for r in range(5)]
    for i in (2, 6):
        x[i] = [subtract(x1[i // 2 + 1, r], y[i][r], x[i - 2], x[i + 2]) for r in range(5)]
    flux = {i: jacobian_times(gas(i + 2), x[i]) for i in (0, 2, 4, 6)}
    flux[8] = [following(value, 1) for value in flux[0]]
    for i in (1, 3, 5, 7):
        sigma, inverse = prm[5, i + 2], prm[6, i + 2]
        x[i] = [
            inverse * (rr[i, p] + sigma * (x[i - 1][p] + x[i + 1][p]) + (flux[i - 1][p] - flux[i + 1][p]))
            for p in range(5)
        ]

    for e in range(2):
        for c in range(2):
            for p in range(5):
                parts = swap_halves(x[4 * e + c][p], x[4 * e + c + 2][p])
                for b in range(2):
                    send_x[pl.ds((2 * b + e) * R + 2 * p + c, 8, stride=4 * R), :] = parts[b]
    exchange(send_x, recv_x, 2)
    arrived(send_x, recv_x, 2)
    for c in range(2):
        for p in range(5):
            parts = [recv_x[pl.ds(h * R + 2 * p + c, 16, stride=2 * R), :] for h in range(2)]
            out_ref[p, c], out_ref[p, c + 2] = swap_halves(*parts)

    for halo in halos:
        halo.wait_send()
    for which, (send, recv) in enumerate(((send_m, recv_m), (send_r, recv_r), (send_x, recv_x))):
        all_of(send, recv, which).wait_send()


def on_device(state, viscosity, residual_other):
    f32 = jnp.float32
    tile = (8, 128)
    buffer = pltpu.VMEM((N * R, 128), f32)
    return pl.pallas_call(
        kernel,
        out_shape=jax.ShapeDtypeStruct(state.shape, f32),
        in_specs=[pl.BlockSpec(memory_space=pl.ANY)] * 3,
        out_specs=pl.BlockSpec(memory_space=pltpu.VMEM),
        scratch_shapes=[
            pltpu.VMEM((5, 4, 32, 128), f32),
            pltpu.VMEM((4, 16, 128), f32),
            pltpu.VMEM((5, 4, 16, 128), f32),
            pltpu.VMEM((5, 32, 128), f32),
            pltpu.VMEM((5, 32, 128), f32),
        ]
        + [buffer] * 6
        + [
            pltpu.VMEM((7, 11) + tile, f32),
            pltpu.VMEM((5, 5, 5) + tile, f32),
            pltpu.VMEM((5, 5, 10) + tile, f32),
            pltpu.VMEM((2, 5, 5) + tile, f32),
            pltpu.VMEM((2, 5, 10) + tile, f32),
            pltpu.VMEM((4, 5, 5) + tile, f32),
            pltpu.VMEM((4, 5, 10) + tile, f32),
            pltpu.VMEM((8, 5) + tile, f32),
            pltpu.VMEM((8, 5) + tile, f32),
            pltpu.SemaphoreType.DMA((3,)),
            pltpu.SemaphoreType.DMA((2,)),
            pltpu.SemaphoreType.DMA((2,)),
            pltpu.SemaphoreType.DMA((3,)),
            pltpu.SemaphoreType.DMA((3,)),
            pltpu.SemaphoreType.DMA((3,)),
        ],
        compiler_params=pltpu.CompilerParams(
            collective_id=0, has_side_effects=True, vmem_limit_bytes=32 * 1024 * 1024
        ),
    )(state, viscosity, residual_other)


def solution(mesh):
    placed = (
        P(None, "stream", "normal", None),
        P("stream", "normal", None),
        P(None, "stream", "normal", None),
    )
    return jax.shard_map(
        on_device,
        mesh=mesh,
        in_specs=placed,
        out_specs=P(None, "stream", "normal", None),
        check_vma=False,
    )
```

time: 467 us -> 32.8 us (0.07)
  the two profiles are of different devices: /device:TPU:102 before, /device:TPU:1 now
where the time goes in v1:
time: 32.8 us; the launch traced here: 32.6 us
  Pallas kernels  29.3 us (89%)
  local copies, waits for them, and re-layouts  3.26 us (10%)
    pallas_call x1, Pallas kernels, on_device(): pl.pallas_call(kernel, out_shape=jax.ShapeDtypeStruct(state.shape, f32),...  29.3 us
    unnamed x7, local copies, waits for them, and re-layouts  3.26 us

profile of v1, /device:TPU:1, one launch (start us, length us, event | category | flops | bytes accessed | tf_op | source)
XLA Modules:
  0.0 32.6 jit_solution(557974472338938559)
XLA Ops:
  0.0 0.0 copy-start
  0.0 0.9 %copy-done = f32[5,4,16,128]{3,2,1,0:T(8,128)S(1)} copy-done((f32[5,4,16,128]{3,2,1,0:T(8,128)S(1)}, f32[5,4,16,128]{3,2,1,0:T(8,128)}, u32[]{:S(2)}) %copy-start) | copy-done | bytes 163864
  0.9 0.0 copy-start.1
  0.9 0.9 %copy-done.1 = f32[5,4,16,128]{3,2,1,0:T(8,128)S(1)} copy-done((f32[5,4,16,128]{3,2,1,0:T(8,128)S(1)}, f32[5,4,16,128]{3,2,1,0:T(8,128)}, u32[]{:S(2)}) %copy-start.1) | copy-done | bytes 163864
  1.8 0.0 copy-start.2
  1.8 0.8 %copy-done.2 = f32[4,16,128]{2,1,0:T(8,128)S(1)} copy-done((f32[4,16,128]{2,1,0:T(8,128)S(1)}, f32[4,16,128]{2,1,0:T(8,128)}, u32[]{:S(2)}) %copy-start.2) | copy-done | bytes 32792
  2.6 29.3 %shard_map.37 = f32[5,4,16,128]{3,2,1,0:T(8,128)S(1)} custom-call(f32[5,4,16,128]{3,2,1,0:T(8,128)S(1)} %copy-done, f32[4,16,128]{2,1,0:T(8,128)S(1)} %copy-done.2, f32[5,4,16,128]{3,2,1,0:T(8,128)S(1)} %copy-done.1), custom_call_target="tpu_custom_call" | custom-call | tf_op jit(solution)/shard_map/pallas_call | solution.py:458
  31.9 0.7 %copy.5 = f32[5,4,16,128]{3,2,1,0:T(8,128)} copy(f32[5,4,16,128]{3,2,1,0:T(8,128)S(1)} %shard_map.37) | data formatting | bytes 327680
Async XLA Ops:
  0.0 0.9 %copy-start = (f32[5,4,16,128]{3,2,1,0:T(8,128)S(1)}, f32[5,4,16,128]{3,2,1,0:T(8,128)}, u32[]{:S(2)}) copy-start(f32[5,4,16,128]{3,2,1,0:T(8,128)} %state_ref.1) | copy-start | bytes 491524
  0.9 0.9 %copy-start.1 = (f32[5,4,16,128]{3,2,1,0:T(8,128)S(1)}, f32[5,4,16,128]{3,2,1,0:T(8,128)}, u32[]{:S(2)}) copy-start(f32[5,4,16,128]{3,2,1,0:T(8,128)} %resid_ref.1) | copy-start | bytes 491524
  1.8 0.8 %copy-start.2 = (f32[4,16,128]{2,1,0:T(8,128)S(1)}, f32[4,16,128]{2,1,0:T(8,128)}, u32[]{:S(2)}) copy-start(f32[4,16,128]{2,1,0:T(8,128)} %visc_ref.1) | copy-start | bytes 98308

commit v2 on v1

--- a/solution.py
+++ b/solution.py
@@ -7,6 +7,7 @@
 
 N = 32
 R = 16
+ROWS = 10
 HALF = 64
 MESH = pl.DeviceIdType.MESH
 
@@ -171,60 +172,82 @@
 
 def kernel(
     state_ref, visc_ref, resid_ref, out_ref,
-    st, vis, res, ss, gg, send_m, recv_m, send_r, recv_r, send_x, recv_x,
-    prm, d1, x1, d2, x2, dp, xp, rr, xx,
+    st, vis, res, halo, gg, send_m, recv_m, send_r, recv_r, send_x, recv_x,
+    prm, d1, x1, d2, x2, dp, xp, rr,
     in_sem, halo_send, halo_recv, a2a_send, a2a_recv, own_sem,
 ):
     me = lax.axis_index("stream")
     z = lax.axis_index("normal")
     z_count = lax.axis_size("normal")
-    z_up = lax.rem(z + 1, z_count)
-    z_down = lax.rem(z + z_count - 1, z_count)
+
+    def load(k, source, target):
+        return pltpu.make_async_copy(source, target, in_sem.at[k])
 
     loads = [
-        pltpu.make_async_copy(state_ref, st.at[:, :, pl.ds(8, 16), :], in_sem.at[0]),
-        pltpu.make_async_copy(visc_ref, vis, in_sem.at[1]),
-        pltpu.make_async_copy(resid_ref, res, in_sem.at[2]),
+        load(0, state_ref, st.at[:, :, pl.ds(8, 16), :]),
+        load(1, visc_ref, vis),
+        load(2, resid_ref, res),
     ]
-    for load in loads:
-        load.start()
+    for each in loads:
+        each.start()
+
+    halo[...] = jnp.zeros_like(halo)
+    for ends in (pl.ds(0, 8), pl.ds(24, 8)):
+        st[:, :, ends, :] = jnp.zeros((5, 4, 8, 128), jnp.float32)
+        gg[:, ends, :] = jnp.zeros((5, 8, 128), jnp.float32)
+
+    has_up, has_down = z < z_count - 1, z > 0
+    px, py, core = me // 8, (me // 2) % 4, me % 2
+
+    def partner(i):
+        return (px + 6 - i // 8) % 4 * 8 + (py + 6 - (i // 2) % 4) % 4 * 2 + (core + i) % 2
+
+    def for_partners(action):
+        def go(i, carry):
+            action(partner(i))
+            return carry
+
+        lax.fori_loop(0, 20, go, 0)
+        lax.fori_loop(21, N, go, 0)
 
     barrier = pltpu.get_barrier_semaphore()
-
-    def greet(k, carry):
-        pl.semaphore_signal(barrier, inc=1, device_id={"stream": lax.rem(me + k, N)}, device_id_type=MESH)
-        return carry
-
-    lax.fori_loop(1, N, greet, 0)
-    for other in (z_up, z_down):
-        pl.semaphore_signal(barrier, inc=1, device_id={"normal": other}, device_id_type=MESH)
+    for_partners(lambda t: pl.semaphore_signal(barrier, inc=1, device_id={"stream": t}, device_id_type=MESH))
+
+    @pl.when(has_up)
+    def _():
+        pl.semaphore_signal(barrier, inc=1, device_id={"normal": z + 1}, device_id_type=MESH)
+
+    @pl.when(has_down)
+    def _():
+        pl.semaphore_signal(barrier, inc=1, device_id={"normal": z - 1}, device_id_type=MESH)
 
     def message(buf, t):
-        return buf.at[pl.ds(pl.multiple_of(t * R, R), R)]
+        return buf.at[pl.ds(pl.multiple_of(t * R, R), ROWS)]
+
+    def send_to(send, recv, which, t):
+        pltpu.make_async_remote_copy(
+            src_ref=message(send, t), dst_ref=message(recv, me),
+            send_sem=a2a_send.at[which], recv_sem=a2a_recv.at[which],
+            device_id={"stream": t}, device_id_type=MESH,
+        ).start()
+
+    def own_copy(send, recv, which):
+        return pltpu.make_async_copy(message(send, me), message(recv, me), own_sem.at[which])
 
     def exchange(send, recv, which):
-        def go(k, carry):
-            t = lax.rem(me + k, N)
-            pltpu.make_async_remote_copy(
-                src_ref=message(send, t), dst_ref=message(recv, me),
-                send_sem=a2a_send.at[which], recv_sem=a2a_recv.at[which],
-                device_id={"stream": t}, device_id_type=MESH,
-            ).start()
-            return carry
-
-        lax.fori_loop(1, N, go, 0)
-        pltpu.make_async_copy(message(send, me), message(recv, me), own_sem.at[which]).start()
+        for_partners(lambda t: send_to(send, recv, which, t))
+        own_copy(send, recv, which).start()
 
     def all_of(send, recv, which):
         return pltpu.make_async_remote_copy(
-            src_ref=send.at[pl.ds(0, (N - 1) * R)], dst_ref=recv.at[pl.ds(0, (N - 1) * R)],
+            src_ref=send.at[pl.ds(0, (N - 1) * ROWS)], dst_ref=recv.at[pl.ds(0, (N - 1) * ROWS)],
             send_sem=a2a_send.at[which], recv_sem=a2a_recv.at[which],
             device_id={"stream": lax.rem(me + 1, N)}, device_id_type=MESH,
         )
 
     def arrived(send, recv, which):
         all_of(send, recv, which).wait_recv()
-        pltpu.make_async_copy(message(send, me), message(recv, me), own_sem.at[which]).wait()
+        own_copy(send, recv, which).wait()
 
     def put(send, row, a, b):
         for h, rows in enumerate(swap_halves(a, b)):
@@ -243,58 +266,95 @@
         for p in range(5):
             put(send_m, 2 * p + c, pair[0][p], pair[1][p])
 
-    pl.semaphore_wait(barrier, N + 1)
-    halos = [
-        pltpu.make_async_remote_copy(
-            src_ref=st.at[:, :, pl.ds(16, 8), :], dst_ref=st.at[:, :, pl.ds(0, 8), :],
-            send_sem=halo_send.at[0], recv_sem=halo_recv.at[0],
-            device_id={"normal": z_up}, device_id_type=MESH,
-        ),
-        pltpu.make_async_remote_copy(
-            src_ref=st.at[:, :, pl.ds(8, 8), :], dst_ref=st.at[:, :, pl.ds(24, 8), :],
-            send_sem=halo_send.at[1], recv_sem=halo_recv.at[1],
-            device_id={"normal": z_down}, device_id_type=MESH,
-        ),
-    ]
-    for halo in halos:
-        halo.start()
+    pl.semaphore_wait(barrier, N - 1 + has_up.astype(jnp.int32) + has_down.astype(jnp.int32))
+    upward = pltpu.make_async_remote_copy(
+        src_ref=state_ref.at[:, :, pl.ds(14, 2), :], dst_ref=halo.at[0, :, :, pl.ds(0, 2), :],
+        send_sem=halo_send.at[0], recv_sem=halo_recv.at[0],
+        device_id={"normal": lax.rem(z + 1, z_count)}, device_id_type=MESH,
+    )
+    downward = pltpu.make_async_remote_copy(
+        src_ref=state_ref.at[:, :, pl.ds(0, 2), :], dst_ref=halo.at[1, :, :, pl.ds(6, 2), :],
+        send_sem=halo_send.at[1], recv_sem=halo_recv.at[1],
+        device_id={"normal": lax.rem(z + z_count - 1, z_count)}, device_id_type=MESH,
+    )
+    pl.when(has_up)(upward.start)
+    pl.when(has_down)(downward.start)
     exchange(send_m, recv_m, 0)
 
+    def flux_of(q):
+        rho, m1, m2, m3, energy = q
+        inverse = 1.0 / rho
+        pressure = 0.4 * (energy - 0.5 * (m1 * m1 + m2 * m2 + m3 * m3) * inverse)
+        v = m2 * inverse
+        return [m2, m1 * v, m2 * v + pressure, m3 * v, (energy + pressure) * v]
+
+    def differences(q, g):
+        second = q(1) - 2.0 * q(0) + q(-1)
+        fourth = q(2) - 4.0 * q(1) + 6.0 * q(0) - 4.0 * q(-1) + q(-2)
+        return second, -40.0 * (g(1) - g(-1)) - 8.0 * fourth
+
     loads[2].wait()
-    for halo in halos:
-        halo.wait_recv()
-    row = lax.broadcasted_iota(jnp.int32, (32, 128), 0)
-    valid = (row >= jnp.where(z == 0, 8, 0)) & (row < jnp.where(z == z_count - 1, 24, 32))
-
-    def right_side(c, carry):
+    for c in range(2):
         pair = []
         for cell in (c, c + 2):
-            q = [st[p, cell] for p in range(5)]
-            rho, m1, m2, m3, energy = q
-            inverse = 1.0 / rho
-            pressure = 0.4 * (energy - 0.5 * (m1 * m1 + m2 * m2 + m3 * m3) * inverse)
-            v = m2 * inverse
-            flux = [m2, m1 * v, m2 * v + pressure, m3 * v, (energy + pressure) * v]
-            sigma = vis[cell]
+            q = [st[p, cell, pl.ds(8, 16), :] for p in range(5)]
+            flux = flux_of(q)
             values = []
             for p in range(5):
-                ss[p] = jnp.where(valid, q[p], 0.0)
-                gg[p] = jnp.where(valid, flux[p], 0.0)
-                s = {d: ss[p, pl.ds(8 + d, 16), :] for d in (-2, -1, 0, 1, 2)}
-                values.append(
-                    res[p, cell]
-                    - 40.0 * (gg[p, pl.ds(9, 16), :] - gg[p, pl.ds(7, 16), :])
-                    + sigma * (s[1] - 2.0 * s[0] + s[-1])
-                    - 8.0 * (s[2] - 4.0 * s[1] + 6.0 * s[0] - 4.0 * s[-1] + s[-2])
+                gg[p, pl.ds(8, 16)] = flux[p]
+                second, rest = differences(
+                    lambda d: st[p, cell, pl.ds(8 + d, 16), :], lambda d: gg[p, pl.ds(8 + d, 16), :]
                 )
+                values.append(res[p, cell] + vis[cell] * second + rest)
             pair.append(values)
         for p in range(5):
             put(send_r, 2 * p + c, pair[0][p], pair[1][p])
+
+    def inner(t):
+        @pl.when((t >= 4) & (t < N - 4))
+        def _():
+            send_to(send_r, recv_r, 1, t)
+
+    for_partners(inner)
+
+    pl.when(has_down)(upward.wait_recv)
+    pl.when(has_up)(downward.wait_recv)
+    index = lax.broadcasted_iota(jnp.int32, (8, 128), 0)
+    for end in range(2):
+        first, offset = 8 * end, -2 + 4 * end
+        real = index < jnp.where(has_up, 8, 6) if end else index >= jnp.where(has_down, 0, 2)
+        for c in range(2):
+            pair = []
+            for cell in (c, c + 2):
+                q = [st[p, cell, pl.ds(6 + 12 * end, 8), :] + halo[end, p, cell] for p in range(5)]
+                flux = flux_of([jnp.where(real, q[0], 1.0)] + q[1:])
+                sigma = vis[cell, pl.ds(first, 8), :]
+                values = []
+                for p in range(5):
+                    g = jnp.where(real, flux[p], 0.0)
+                    second, rest = differences(lambda d: roll_rows(q[p], -d), lambda d: roll_rows(g, -d))
+                    values.append(
+                        res[p, cell, pl.ds(first, 8), :]
+                        + sigma * roll_rows(second, offset)
+                        + roll_rows(rest, offset)
+                    )
+                pair.append(values)
+            for p in range(5):
+                for h, rows in enumerate(swap_halves(pair[0][p], pair[1][p])):
+                    at = (28 * end + h) * R + 2 * p + c
+                    send_r[pl.ds(at, 2, stride=2 * R), :] = rows[6 * end : 6 * end + 2]
+
+    def outer(i, carry):
+        t = jnp.where(i < 4, i, i + N - 8)
+
+        @pl.when(t != me)
+        def _():
+            send_to(send_r, recv_r, 1, t)
+
         return carry
 
-    for c in range(2):
-        right_side(c, 0)
-    exchange(send_r, recv_r, 1)
+    lax.fori_loop(0, 8, outer, 0)
+    own_copy(send_r, recv_r, 1).start()
 
     def get(recv, row, e):
         return swap_halves(*(recv[pl.ds((2 * b + e) * R + row, 8, stride=4 * R), :] for b in range(2)))
@@ -378,8 +438,8 @@
     q, _ = place((5, 8, 128))
     other = [jnp.where(q < 4, xp[3, r, pl.ds(5, 5)], xp[3, r, pl.ds(0, 5)]) for r in range(5)]
     other = solve_rows(lu, recip, other)
-    partner = [roll_rows(x, 4) for x in other]
-    last, last_recip = factor_rows([identity[r] - row_times(other[r], partner) for r in range(5)])
+    facing = [roll_rows(x, 4) for x in other]
+    last, last_recip = factor_rows([identity[r] - row_times(other[r], facing) for r in range(5)])
 
     arrived(send_r, recv_r, 1)
     for e in range(2):
@@ -445,8 +505,8 @@
             parts = [recv_x[pl.ds(h * R + 2 * p + c, 16, stride=2 * R), :] for h in range(2)]
             out_ref[p, c], out_ref[p, c + 2] = swap_halves(*parts)
 
-    for halo in halos:
-        halo.wait_send()
+    pl.when(has_up)(upward.wait_send)
+    pl.when(has_down)(downward.wait_send)
     for which, (send, recv) in enumerate(((send_m, recv_m), (send_r, recv_r), (send_x, recv_x))):
         all_of(send, recv, which).wait_send()
 
@@ -458,16 +518,16 @@
     return pl.pallas_call(
         kernel,
         out_shape=jax.ShapeDtypeStruct(state.shape, f32),
-        in_specs=[pl.BlockSpec(memory_space=pl.ANY)] * 3,
+        in_specs=[pl.BlockSpec(memory_space=pltpu.HBM)] * 3,
         out_specs=pl.BlockSpec(memory_space=pltpu.VMEM),
         scratch_shapes=[
             pltpu.VMEM((5, 4, 32, 128), f32),
             pltpu.VMEM((4, 16, 128), f32),
             pltpu.VMEM((5, 4, 16, 128), f32),
-            pltpu.VMEM((5, 32, 128), f32),
+            pltpu.VMEM((2, 5, 4, 8, 128), f32),
             pltpu.VMEM((5, 32, 128), f32),
         ]
-        + [buffer] * 6
+        + [buffer, buffer, pltpu.VMEM((3 * N * R // 2, 128), f32), buffer, buffer, buffer]
         + [
             pltpu.VMEM((7, 11) + tile, f32),
             pltpu.VMEM((5, 5, 5) + tile, f32),
@@ -476,7 +536,6 @@
             pltpu.VMEM((2, 5, 10) + tile, f32),
             pltpu.VMEM((4, 5, 5) + tile, f32),
             pltpu.VMEM((4, 5, 10) + tile, f32),
-            pltpu.VMEM((8, 5) + tile, f32),
             pltpu.VMEM((8, 5) + tile, f32),
             pltpu.SemaphoreType.DMA((3,)),
             pltpu.SemaphoreType.DMA((2,)),
@@ -488,7 +547,7 @@
         compiler_params=pltpu.CompilerParams(
             collective_id=0, has_side_effects=True, vmem_limit_bytes=32 * 1024 * 1024
         ),
-    )(state, viscosity, residual_other)
+    )(*(pltpu.with_memory_space_constraint(x, pltpu.HBM) for x in (state, viscosity, residual_other)))
 
 
 def solution(mesh):

time: 32.8 us -> 22.7 us (0.69)
  Pallas kernels: 29.3 us -> 21.6 us
  local copies, waits for them, and re-layouts: 3.26 us -> 0.67 us
    pallas_call x1, Pallas kernels: 29.3 us -> 21.6 us  [on_device(): pl.pallas_call(kernel, out_shape=jax.ShapeDtypeStruct(state.shape, f32),...]
    unnamed x7 -> x1, local copies, waits for them, and re-layouts: 3.26 us -> 0.67 us
where the time goes in v2:
time: 22.7 us; the launch traced here: 22.3 us
  Pallas kernels  21.6 us (95%)
  local copies, waits for them, and re-layouts  0.67 us (3%)
    pallas_call x1, Pallas kernels, on_device(): pl.pallas_call(kernel, out_shape=jax.ShapeDtypeStruct(state.shape, f32),...  21.6 us
    unnamed x1, local copies, waits for them, and re-layouts  0.67 us

profile of v2, /device:TPU:1, one launch (start us, length us, event | category | flops | bytes accessed | tf_op | source)
XLA Modules:
  0.0 22.3 jit_solution(4144390625141086962)
XLA Ops:
  0.0 21.6 %shard_map.37 = f32[5,4,16,128]{3,2,1,0:T(8,128)S(1)} custom-call(f32[5,4,16,128]{3,2,1,0:T(8,128)} %state_ref.1, f32[4,16,128]{2,1,0:T(8,128)} %visc_ref.1, f32[5,4,16,128]{3,2,1,0:T(8,128)} %resid_ref.1), custom_call_target="tpu_custom_call" | custom-call | tf_op jit(solution)/shard_map/pallas_call | solution.py:518
  21.6 0.7 %copy.5 = f32[5,4,16,128]{3,2,1,0:T(8,128)} copy(f32[5,4,16,128]{3,2,1,0:T(8,128)S(1)} %shard_map.37) | data formatting | bytes 327680

commit v3 on v2

v3 whole, which is shorter than its diff:
```python
import jax
import jax.numpy as jnp
from jax import lax
from jax.experimental import pallas as pl
from jax.experimental.pallas import tpu as pltpu
from jax.sharding import PartitionSpec as P

N = 32
R = 16
ROWS = (10, 5, 5)
HALF = 64
MESH = pl.DeviceIdType.MESH


def roll_lanes(x):
    return pltpu.roll(x, HALF, axis=x.ndim - 1)


def roll_rows(x, by):
    return pltpu.roll(x, by % 8, axis=x.ndim - 2)


def swap_halves(a, b):
    low = lax.broadcasted_iota(jnp.int32, a.shape, a.ndim - 1) < HALF
    return jnp.where(low, a, roll_lanes(b)), jnp.where(low, roll_lanes(a), b)


def place(shape):
    q = lax.broadcasted_iota(jnp.int32, shape, len(shape) - 2)
    b = lax.broadcasted_iota(jnp.int32, shape, len(shape) - 1) >= HALF
    return q, b


def previous(x, by):
    q, b = place(x.shape)
    if by == 1:
        moved = roll_lanes(jnp.where(b, roll_rows(x, 1), x))
        return jnp.where((q == 0) & ~b, 0.0, moved)
    return jnp.where(q < by // 2, 0.0, roll_rows(x, by // 2))


def following(x, by):
    q, b = place(x.shape)
    if by == 1:
        moved = roll_lanes(jnp.where(b, x, roll_rows(x, -1)))
        return jnp.where((q == 7) & b, 0.0, moved)
    return jnp.where(q >= 8 - by // 2, 0.0, roll_rows(x, -(by // 2)))


def jacobian_rows(u, v, w, h, k):
    return [
        [None, 1.0, None, None, None],
        [0.4 * k - u * u, 1.6 * u, -0.4 * v, -0.4 * w, 0.4],
        [-u * v, v, u, None, None],
        [-u * w, w, None, u, None],
        [u * (0.4 * k - h), h - 0.4 * u * u, -0.4 * u * v, -0.4 * u * w, 1.4 * u],
    ]


def jacobian_times(prm, m):
    u, v, w, h, k = prm
    t = m[1] - u * m[0]
    p = 0.4 * (k * m[0] - u * m[1] - v * m[2] - w * m[3] + m[4])
    return [
        m[1],
        p + u * (m[1] + t),
        v * t + u * m[2],
        w * t + u * m[3],
        u * (p + m[4]) + h * t,
    ]


def row_times_jacobian(g, prm, shift):
    u, v, w, h, k = prm
    e = g[0]
    for value, factor in ((g[1], u), (g[2], v), (g[3], w), (g[4], h)):
        if value is not None:
            e = value * factor if e is None else e + value * factor
    p = g[1] if g[4] is None else g[1] + u * g[4]
    p = 0.4 * p
    s = u + shift

    def part(index, other):
        return other if g[index] is None else s * g[index] + other

    return [
        part(0, k * p - u * e),
        part(1, e - u * p),
        part(2, -(v * p)),
        part(3, -(w * p)),
        part(4, p),
    ]


def scaled(rows, shift, factor):
    out = []
    for r in range(5):
        row = []
        for c in range(5):
            value = rows[r][c]
            if r == c:
                value = shift if value is None else value + shift
            row.append(None if value is None else value * factor)
        out.append(row)
    return out


def plus(a, b):
    if a is None:
        return b
    return a if b is None else a + b


def shifted(prm, m, shift):
    return [a + shift * b for a, b in zip(jacobian_times(prm, m), m)]


def diagonal_rows(left, right, here, before, sigma, after):
    rows = []
    for r in range(5):
        own = row_times_jacobian([plus(left[r][c], right[r][c]) for c in range(5)], here, 0.0)
        for c in range(5):
            if left[r][c] is not None:
                own[c] = own[c] + (after * right[r][c] - before * left[r][c])
        own[r] = own[r] + (1.0 + 2.0 * sigma)
        rows.append(own)
    return rows


def factor_rows(rows):
    rows = list(rows)
    recip = []
    for p in range(5):
        rec = 1.0 / rows[p][p]
        recip.append(rec)
        for r in range(p + 1, 5):
            weight = rows[r][p] * rec
            tail = rows[r][p + 1 :] - weight[None] * rows[p][p + 1 :] if p < 4 else None
            parts = [rows[r][:p], weight[None], tail] if p else [weight[None], tail]
            rows[r] = jnp.concatenate(parts, axis=0)
    return rows, recip


def solve_rows(lu, recip, right):
    x = list(right)
    for p in range(5):
        for r in range(p + 1, 5):
            x[r] = x[r] - lu[r][p] * x[p]
    for p in range(4, -1, -1):
        x[p] = x[p] * recip[p]
        for r in range(p):
            x[r] = x[r] - lu[r][p] * x[p]
    return x


def identity(like):
    one, zero = jnp.ones_like(like), jnp.zeros_like(like)
    return [jnp.stack([one if r == c else zero for c in range(5)]) for r in range(5)]


def inverse_of(rows):
    return solve_rows(*factor_rows(rows), identity(rows[0][0]))


def normalise(d_ref, x_ref, s):
    rows = [d_ref[s, r] for r in range(5)]
    unit = identity(rows[0][0])
    x = solve_rows(*factor_rows(rows), [jnp.concatenate([x_ref[s, r], unit[r]], axis=0) for r in range(5)])
    for r in range(5):
        x_ref[s, r], d_ref[s, r] = x[r][:10], x[r][10:]


def times(rows, m):
    return [row_times(row, m) for row in rows]


def row_times(row, others):
    first = row[0] * others[0] + row[1] * others[1]
    return first + (row[2] * others[2] + row[3] * others[3]) + row[4] * others[4]


def combine(own, diagonal, before, after, d_ref, x_ref, s):
    for r in range(5):
        left = row_times(own[r][:5], before)
        right = row_times(own[r][5:], after)
        d_ref[s, r] = diagonal[r] - left[5:] - right[:5]
        x_ref[s, r] = jnp.concatenate([-left[:5], -right[5:]], axis=0)


def subtract(own, r, before, after):
    return r - (row_times(own[:5], before) + row_times(own[5:], after))


def kernel(
    state_ref, visc_ref, resid_ref, out_ref,
    st, vis, res, ro, halo, gg, send_m, recv_m, send_r, recv_r, send_x, recv_x,
    prm, d1, l1, d2, l2, dp, lp,
    in_sem, halo_send, halo_recv, a2a_send, a2a_recv, own_sem,
):
    me = lax.axis_index("stream")
    z = lax.axis_index("normal")
    z_count = lax.axis_size("normal")

    def load(k, source, target):
        return pltpu.make_async_copy(source, target, in_sem.at[k])

    loads = [
        load(0, state_ref, st.at[:, :, pl.ds(8, 16), :]),
        load(1, visc_ref, vis),
        load(2, resid_ref, res),
    ]
    for each in loads:
        each.start()

    halo[...] = jnp.zeros_like(halo)
    has_up, has_down = z < z_count - 1, z > 0
    px, py, core = me // 8, (me // 2) % 4, me % 2

    def partner(i):
        return (px + 6 - i // 8) % 4 * 8 + (py + 6 - (i // 2) % 4) % 4 * 2 + (core + i) % 2

    def for_partners(action):
        def go(i, carry):
            action(partner(i))
            return carry

        lax.fori_loop(0, 20, go, 0)
        lax.fori_loop(21, N, go, 0)

    barrier = pltpu.get_barrier_semaphore()

    @pl.when(has_up)
    def _():
        pl.semaphore_signal(barrier, inc=1, device_id={"normal": z + 1}, device_id_type=MESH)

    @pl.when(has_down)
    def _():
        pl.semaphore_signal(barrier, inc=1, device_id={"normal": z - 1}, device_id_type=MESH)

    for_partners(lambda t: pl.semaphore_signal(barrier, inc=1, device_id={"stream": t}, device_id_type=MESH))
    for ends in (pl.ds(0, 8), pl.ds(24, 8)):
        st[:, :, ends, :] = jnp.zeros((5, 4, 8, 128), jnp.float32)
        gg[:, ends, :] = jnp.zeros((5, 8, 128), jnp.float32)

    slot = lax.rem(me + N - 4, N)

    def message(buf, which, t):
        return buf.at[pl.ds(pl.multiple_of(t * R, R), ROWS[which])]

    def slot_of(t):
        return lax.rem(t + N - 4, N)

    def there(send, recv, which, t):
        if which == 2:
            return message(send, which, t), message(recv, which, slot)
        return message(send, which, slot_of(t)), message(recv, which, me)

    def own_copy(send, recv, which):
        return pltpu.make_async_copy(*there(send, recv, which, me), own_sem.at[which])

    def send_to(send, recv, which, t):
        source, target = there(send, recv, which, t)
        pltpu.make_async_remote_copy(
            src_ref=source, dst_ref=target,
            send_sem=a2a_send.at[which], recv_sem=a2a_recv.at[which],
            device_id={"stream": t}, device_id_type=MESH,
        ).start()

    def exchange(send, recv, which):
        for_partners(lambda t: send_to(send, recv, which, t))
        own_copy(send, recv, which).start()

    def all_of(send, recv, which):
        return pltpu.make_async_remote_copy(
            src_ref=send.at[pl.ds(0, (N - 1) * ROWS[which])], dst_ref=recv.at[pl.ds(0, (N - 1) * ROWS[which])],
            send_sem=a2a_send.at[which], recv_sem=a2a_recv.at[which],
            device_id={"stream": lax.rem(me + 1, N)}, device_id_type=MESH,
        )

    def arrived(send, recv, which):
        all_of(send, recv, which).wait_recv()
        own_copy(send, recv, which).wait()

    def put(send, row, a, b):
        for h, rows in enumerate(swap_halves(a, b)):
            send[pl.ds(h * R + row, 16, stride=2 * R), :] = rows

    loads[0].wait()
    loads[1].wait()
    gas_own, sig = [], [vis[cell] for cell in range(4)]
    for cell in range(4):
        rho, m1, m2, m3, energy = (st[p, cell, pl.ds(8, 16), :] for p in range(5))
        inverse = 1.0 / rho
        u, v, w = m1 * inverse, m2 * inverse, m3 * inverse
        k = 0.5 * (u * u + v * v + w * w)
        gas_own.append((u, v, w, 1.4 * energy * inverse - 0.4 * k, k))
    for c in range(2):
        for p in range(4):
            put(send_m, 2 * p + c, gas_own[c][p], gas_own[c + 2][p])
        put(send_m, 8 + c, sig[c], sig[c + 2])

    def flux_of(q):
        rho, m1, m2, m3, energy = q
        inverse = 1.0 / rho
        pressure = 0.4 * (energy - 0.5 * (m1 * m1 + m2 * m2 + m3 * m3) * inverse)
        v = m2 * inverse
        return [m2, m1 * v, m2 * v + pressure, m3 * v, (energy + pressure) * v]

    loads[2].wait()
    for cell in range(4):
        flux = flux_of([st[p, cell, pl.ds(8, 16), :] for p in range(5)])
        for p in range(5):
            gg[p, pl.ds(8, 16)] = flux[p]
            s = {d: st[p, cell, pl.ds(8 + d, 16), :] for d in (-2, -1, 0, 1, 2)}
            g = {d: gg[p, pl.ds(8 + d, 16), :] for d in (-1, 1)}
            ro[cell, p] = (
                res[p, cell]
                - 40.0 * (g[1] - g[-1])
                + vis[cell] * (s[1] - 2.0 * s[0] + s[-1])
                - 8.0 * (s[2] - 4.0 * s[1] + 6.0 * s[0] - 4.0 * s[-1] + s[-2])
            )

    inv1, inv3 = (1.0 / (1.0 + 2.0 * sig[cell]) for cell in (1, 3))
    own_inverse = inverse_of([
        jnp.stack(values)
        for values in diagonal_rows(
            scaled(jacobian_rows(*gas_own[1]), sig[2], inv1), scaled(jacobian_rows(*gas_own[3]), -sig[2], inv3),
            gas_own[2], sig[1], sig[2], sig[3],
        )
    ])

    def around(y1, x2, y3):
        flux = jacobian_times(gas_own[2], x2)
        x1 = [y1[p] - inv1 * (flux[p] - sig[1] * x2[p]) for p in range(5)]
        return x1, [y3[p] + inv3 * (flux[p] + sig[3] * x2[p]) for p in range(5)]

    def to_cell_2(y1, y3):
        a, b = shifted(gas_own[1], y1, sig[2]), shifted(gas_own[3], y3, -sig[2])
        return [a[p] - b[p] for p in range(5)]

    def condensed():
        y1, y3 = [inv1 * ro[1, p] for p in range(5)], [inv3 * ro[3, p] for p in range(5)]
        t = to_cell_2(y1, y3)
        x2 = times(own_inverse, [ro[2, p] + t[p] for p in range(5)])
        x1, x3 = around(y1, x2, y3)
        t = shifted(gas_own[1], x1, -sig[0])
        return [ro[0, p] - t[p] for p in range(5)], x3, y1, x2, y3

    rest, x3, *_ = condensed()
    for p in range(5):
        put(send_r, p, rest[p], x3[p])

    pl.semaphore_wait(barrier, N - 1 + has_up.astype(jnp.int32) + has_down.astype(jnp.int32))
    upward = pltpu.make_async_remote_copy(
        src_ref=state_ref.at[:, :, pl.ds(14, 2), :], dst_ref=halo.at[:, :, pl.ds(0, 2), :],
        send_sem=halo_send.at[0], recv_sem=halo_recv.at[0],
        device_id={"normal": lax.rem(z + 1, z_count)}, device_id_type=MESH,
    )
    downward = pltpu.make_async_remote_copy(
        src_ref=state_ref.at[:, :, pl.ds(0, 2), :], dst_ref=halo.at[:, :, pl.ds(6, 2), :],
        send_sem=halo_send.at[1], recv_sem=halo_recv.at[1],
        device_id={"normal": lax.rem(z + z_count - 1, z_count)}, device_id_type=MESH,
    )
    pl.when(has_up)(upward.start)
    pl.when(has_down)(downward.start)
    exchange(send_m, recv_m, 0)

    def inner(t):
        @pl.when(t >= 8)
        def _():
            send_to(send_r, recv_r, 1, t)

    for_partners(inner)

    pl.when(has_down)(upward.wait_recv)
    pl.when(has_up)(downward.wait_recv)
    index = lax.broadcasted_iota(jnp.int32, (8, 128), 0)
    low = index < 4
    edge = (index == 0) | (index == 7)

    def inward(plane):
        return jnp.where(low, roll_rows(plane, -1), roll_rows(plane, 1))

    for cell in range(4):
        q = [halo[p, cell] for p in range(5)]
        flux = flux_of([jnp.where(q[0] > 0.0, q[0], 1.0)] + q[1:])
        factor = 32.0 + jnp.where(low, vis[cell, pl.ds(0, 8), :], vis[cell, pl.ds(8, 8), :])
        for p in range(5):
            change = jnp.where(edge, factor * inward(q[p]) + jnp.where(low, 40.0, -40.0) * inward(flux[p]), 0.0)
            change = change - 8.0 * q[p]
            ro[cell, p, pl.ds(0, 8), :] = ro[cell, p, pl.ds(0, 8), :] + jnp.where(low, change, 0.0)
            ro[cell, p, pl.ds(8, 8), :] = ro[cell, p, pl.ds(8, 8), :] + jnp.where(low, 0.0, change)
    rest, x3, y1, x2, y3 = condensed()
    for p in range(5):
        for h, rows in enumerate(swap_halves(rest[p], x3[p])):
            for end in range(2):
                send_r[pl.ds((28 * end + h) * R + p, 2, stride=2 * R), :] = rows[14 * end : 14 * end + 2]

    def outer(t, carry):
        @pl.when(t != me)
        def _():
            send_to(send_r, recv_r, 1, t)

        return carry

    lax.fori_loop(0, 8, outer, 0)
    own_copy(send_r, recv_r, 1).start()

    def get(recv, row, e):
        return swap_halves(*(recv[pl.ds((2 * b + e) * R + row, 8, stride=4 * R), :] for b in range(2)))

    arrived(send_m, recv_m, 0)
    for e in range(2):
        for c in range(2):
            both = [get(recv_m, 2 * p + c, e) for p in range(5)]
            for side in range(2):
                u, v, w, h, sigma = (both[p][side] for p in range(5))
                k = 0.5 * (u * u + v * v + w * w)
                cell = 4 * e + c + 2 * side
                values = (u, v, w, h, k, sigma, 1.0 / (1.0 + 2.0 * sigma))
                for p in range(7):
                    prm[p, cell + 2] = values[p]
                    if cell >= 6:
                        prm[p, cell - 6] = previous(values[p], 1)
                    if cell == 0:
                        prm[p, 10] = following(values[p], 1)

    def gas(place_):
        return tuple(prm[p, place_] for p in range(5))

    def level_1(i, carry):
        at = 2 * i + 2
        sigma, before, after = prm[5, at], prm[5, at - 1], prm[5, at + 1]
        left = scaled(jacobian_rows(*gas(at - 1)), sigma, prm[6, at - 1])
        right = scaled(jacobian_rows(*gas(at + 1)), -sigma, prm[6, at + 1])
        here, far_left, far_right = gas(at), gas(at - 2), gas(at + 2)
        own = diagonal_rows(left, right, here, before, sigma, after)
        for r in range(5):
            lower = row_times_jacobian(left[r], far_left, before)
            upper = row_times_jacobian(right[r], far_right, -after)
            for c in range(5):
                d1[i + 1, r, c] = own[r][c]
                l1[i + 1, r, c] = -lower[c]
                l1[i + 1, r, 5 + c] = -upper[c]
        return carry

    lax.fori_loop(0, 4, level_1, 0)

    def level_2_normalise(i, carry):
        normalise(d1, l1, 2 * i + 2)
        return carry

    lax.fori_loop(0, 2, level_2_normalise, 0)
    for r in range(5):
        l1[0, r] = previous(l1[4, r], 1)

    def rows_of(ref, s):
        return [ref[s, r] for r in range(5)]

    def level_2_combine(i, carry):
        s = 2 * i + 1
        combine(rows_of(l1, s), rows_of(d1, s), rows_of(l1, s - 1), rows_of(l1, s + 1), d2, l2, i)
        return carry

    lax.fori_loop(0, 2, level_2_combine, 0)

    normalise(d2, l2, 1)
    combine(
        rows_of(l2, 0), rows_of(d2, 0), [previous(l2[1, r], 1) for r in range(5)], rows_of(l2, 1), dp, lp, 0
    )

    unit = identity(jnp.ones((8, 128), jnp.float32))
    for step in range(3):
        normalise(dp, lp, step)
        own = rows_of(lp, step)
        combine(
            own, unit, [previous(x, 2**step) for x in own], [following(x, 2**step) for x in own],
            dp, lp, step + 1,
        )
    q, _ = place((5, 8, 128))
    other = [jnp.where(q < 4, lp[3, r, pl.ds(5, 5)], lp[3, r, pl.ds(0, 5)]) for r in range(5)]
    both = solve_rows(*factor_rows(rows_of(dp, 3)), [jnp.concatenate([other[r], unit[r]], axis=0) for r in range(5)])
    other, fourth = [row[:5] for row in both], [row[5:] for row in both]
    facing = [roll_rows(x, 4) for x in other]
    last = inverse_of([unit[r] - row_times(other[r], facing) for r in range(5)])

    arrived(send_r, recv_r, 1)
    parts = [[get(recv_r, p, e) for p in range(5)] for e in range(2)]
    inside = [[parts[e][p][1] for p in range(5)] for e in range(2)]
    four = {}
    for i, before in ((0, [previous(value, 1) for value in inside[1]]), (4, inside[0])):
        t = shifted(gas(i + 1), before, prm[5, i + 2])
        four[i] = [parts[i // 4][p][0] + t[p] for p in range(5)]
    y = {}
    y[4] = times(rows_of(d2, 1), four[4])
    before = [previous(value, 1) for value in y[4]]
    b = [subtract(l2[0, r], four[0][r], before, y[4]) for r in range(5)]
    for step in range(3):
        b = times(rows_of(dp, step), b)
        before = [previous(value, 2**step) for value in b]
        after = [following(value, 2**step) for value in b]
        b = [subtract(lp[step, r], b[r], before, after) for r in range(5)]
    b = times(fourth, b)
    paired = [roll_rows(value, 4) for value in b]
    b = [b[r] - row_times(other[r], paired) for r in range(5)]
    x = {0: times(last, b)}
    x[8] = [following(value, 1) for value in x[0]]
    x[4] = [subtract(l2[1, r], y[4][r], x[0], x[8]) for r in range(5)]

    for e in range(2):
        beyond = shifted(gas(4 * e + 6), x[4 * e + 4], -prm[5, 4 * e + 5])
        for p in range(5):
            for b, rows in enumerate(swap_halves(x[4 * e][p], beyond[p])):
                send_x[pl.ds((2 * b + e) * R + p, 8, stride=4 * R), :] = rows
    exchange(send_x, recv_x, 2)
    arrived(send_x, recv_x, 2)
    both = [swap_halves(*(recv_x[pl.ds(h * R + p, 16, stride=2 * R), :] for h in range(2))) for p in range(5)]
    x0 = [both[p][0] for p in range(5)]
    after = [inv3 * both[p][1] for p in range(5)]
    before = [inv1 * value for value in shifted(gas_own[0], x0, sig[1])]
    t = times(own_inverse, to_cell_2(before, [-value for value in after]))
    x2 = [x2[p] + t[p] for p in range(5)]
    x1, x3 = around([y1[p] + before[p] for p in range(5)], x2, [y3[p] - after[p] for p in range(5)])
    for p in range(5):
        out_ref[p, 0], out_ref[p, 1], out_ref[p, 2], out_ref[p, 3] = x0[p], x1[p], x2[p], x3[p]

    pl.when(has_up)(upward.wait_send)
    pl.when(has_down)(downward.wait_send)
    for which, (send, recv) in enumerate(((send_m, recv_m), (send_r, recv_r), (send_x, recv_x))):
        all_of(send, recv, which).wait_send()


def on_device(state, viscosity, residual_other):
    f32 = jnp.float32
    tile = (8, 128)
    buffer = pltpu.VMEM((N * R, 128), f32)
    return pl.pallas_call(
        kernel,
        out_shape=jax.ShapeDtypeStruct(state.shape, f32),
        in_specs=[pl.BlockSpec(memory_space=pltpu.HBM)] * 3,
        out_specs=pl.BlockSpec(memory_space=pltpu.VMEM),
        scratch_shapes=[
            pltpu.VMEM((5, 4, 32, 128), f32),
            pltpu.VMEM((4, 16, 128), f32),
            pltpu.VMEM((5, 4, 16, 128), f32),
            pltpu.VMEM((4, 5, 16, 128), f32),
            pltpu.VMEM((5, 4, 8, 128), f32),
            pltpu.VMEM((5, 32, 128), f32),
        ]
        + [buffer, buffer, pltpu.VMEM((3 * N * R // 2, 128), f32), buffer, buffer, buffer]
        + [
            pltpu.VMEM((7, 11) + tile, f32),
            pltpu.VMEM((5, 5, 5) + tile, f32),
            pltpu.VMEM((5, 5, 10) + tile, f32),
            pltpu.VMEM((2, 5, 5) + tile, f32),
            pltpu.VMEM((2, 5, 10) + tile, f32),
            pltpu.VMEM((4, 5, 5) + tile, f32),
            pltpu.VMEM((4, 5, 10) + tile, f32),
            pltpu.SemaphoreType.DMA((3,)),
            pltpu.SemaphoreType.DMA((2,)),
            pltpu.SemaphoreType.DMA((2,)),
            pltpu.SemaphoreType.DMA((3,)),
            pltpu.SemaphoreType.DMA((3,)),
            pltpu.SemaphoreType.DMA((3,)),
        ],
        compiler_params=pltpu.CompilerParams(
            collective_id=0, has_side_effects=True, vmem_limit_bytes=32 * 1024 * 1024
        ),
    )(*(pltpu.with_memory_space_constraint(x, pltpu.HBM) for x in (state, viscosity, residual_other)))


def solution(mesh):
    placed = (
        P(None, "stream", "normal", None),
        P("stream", "normal", None),
        P(None, "stream", "normal", None),
    )
    return jax.shard_map(
        on_device,
        mesh=mesh,
        in_specs=placed,
        out_specs=P(None, "stream", "normal", None),
        check_vma=False,
    )
```

time: 22.7 us -> 21.8 us (0.960)
  the two profiles are of different devices: /device:TPU:1 before, /device:TPU:103 now
where the time goes in v3:
time: 21.8 us; the launch traced here: 21.7 us
  Pallas kernels  21.1 us (97%)
  local copies, waits for them, and re-layouts  0.67 us (3%)
    pallas_call x1, Pallas kernels, on_device(): pl.pallas_call(kernel, out_shape=jax.ShapeDtypeStruct(state.shape, f32),...  21.1 us
    unnamed x1, local copies, waits for them, and re-layouts  0.67 us

profile of v3, /device:TPU:103, one launch (start us, length us, event | category | flops | bytes accessed | tf_op | source)
XLA Modules:
  0.0 21.7 jit_solution(15798817410308994077)
XLA Ops:
  0.0 21.1 %shard_map.37 = f32[5,4,16,128]{3,2,1,0:T(8,128)S(1)} custom-call(f32[5,4,16,128]{3,2,1,0:T(8,128)} %state_ref.1, f32[4,16,128]{2,1,0:T(8,128)} %visc_ref.1, f32[5,4,16,128]{3,2,1,0:T(8,128)} %resid_ref.1), custom_call_target="tpu_custom_call" | custom-call | tf_op jit(solution)/shard_map/pallas_call | solution.py:537
  21.1 0.7 %copy.5 = f32[5,4,16,128]{3,2,1,0:T(8,128)} copy(f32[5,4,16,128]{3,2,1,0:T(8,128)S(1)} %shard_map.37) | data formatting | bytes 327680

commit v4 on v3

--- a/solution.py
+++ b/solution.py
@@ -193,7 +193,7 @@
 
 def kernel(
     state_ref, visc_ref, resid_ref, out_ref,
-    st, vis, res, ro, halo, gg, send_m, recv_m, send_r, recv_r, send_x, recv_x,
+    st, vis, res, ro, halo, away, gg, send_m, recv_m, send_r, recv_r, send_x, recv_x,
     prm, d1, l1, d2, l2, dp, lp,
     in_sem, halo_send, halo_recv, a2a_send, a2a_recv, own_sem,
 ):
@@ -214,18 +214,15 @@
 
     halo[...] = jnp.zeros_like(halo)
     has_up, has_down = z < z_count - 1, z > 0
-    px, py, core = me // 8, (me // 2) % 4, me % 2
-
-    def partner(i):
-        return (px + 6 - i // 8) % 4 * 8 + (py + 6 - (i // 2) % 4) % 4 * 2 + (core + i) % 2
+    along_x = [lax.rem(me // 8 + d, 4) * 8 for d in range(4)]
+    along_y = [lax.rem(lax.rem(me // 2, 4) + d, 4) * 2 for d in range(4)]
+    cores = [lax.rem(me, 2), 1 - lax.rem(me, 2)]
+    steps = [(dx, dy, dc) for dx in range(4) for dy in range(4) for dc in (1, 0) if dx or dy or dc]
+    steps.sort(key=lambda d: -(min(d[0], 4 - d[0]) + min(d[1], 4 - d[1])))
 
     def for_partners(action):
-        def go(i, carry):
-            action(partner(i))
-            return carry
-
-        lax.fori_loop(0, 20, go, 0)
-        lax.fori_loop(21, N, go, 0)
+        for dx, dy, dc in steps:
+            action(along_x[dx] + along_y[dy] + cores[dc])
 
     barrier = pltpu.get_barrier_semaphore()
 
@@ -287,6 +284,10 @@
 
     loads[0].wait()
     loads[1].wait()
+    for p in range(5):
+        for cell in range(4):
+            away[0, p, cell] = st[p, cell, pl.ds(22, 2), :]
+            away[1, p, cell] = st[p, cell, pl.ds(8, 2), :]
     gas_own, sig = [], [vis[cell] for cell in range(4)]
     for cell in range(4):
         rho, m1, m2, m3, energy = (st[p, cell, pl.ds(8, 16), :] for p in range(5))
@@ -298,6 +299,21 @@
         for p in range(4):
             put(send_m, 2 * p + c, gas_own[c][p], gas_own[c + 2][p])
         put(send_m, 8 + c, sig[c], sig[c + 2])
+
+    pl.semaphore_wait(barrier, N - 1 + has_up.astype(jnp.int32) + has_down.astype(jnp.int32))
+    upward = pltpu.make_async_remote_copy(
+        src_ref=away.at[0], dst_ref=halo.at[0],
+        send_sem=halo_send.at[0], recv_sem=halo_recv.at[0],
+        device_id={"normal": lax.rem(z + 1, z_count)}, device_id_type=MESH,
+    )
+    downward = pltpu.make_async_remote_copy(
+        src_ref=away.at[1], dst_ref=halo.at[1],
+        send_sem=halo_send.at[1], recv_sem=halo_recv.at[1],
+        device_id={"normal": lax.rem(z + z_count - 1, z_count)}, device_id_type=MESH,
+    )
+    pl.when(has_up)(upward.start)
+    pl.when(has_down)(downward.start)
+    exchange(send_m, recv_m, 0)
 
     def flux_of(q):
         rho, m1, m2, m3, energy = q
@@ -350,21 +366,6 @@
     for p in range(5):
         put(send_r, p, rest[p], x3[p])
 
-    pl.semaphore_wait(barrier, N - 1 + has_up.astype(jnp.int32) + has_down.astype(jnp.int32))
-    upward = pltpu.make_async_remote_copy(
-        src_ref=state_ref.at[:, :, pl.ds(14, 2), :], dst_ref=halo.at[:, :, pl.ds(0, 2), :],
-        send_sem=halo_send.at[0], recv_sem=halo_recv.at[0],
-        device_id={"normal": lax.rem(z + 1, z_count)}, device_id_type=MESH,
-    )
-    downward = pltpu.make_async_remote_copy(
-        src_ref=state_ref.at[:, :, pl.ds(0, 2), :], dst_ref=halo.at[:, :, pl.ds(6, 2), :],
-        send_sem=halo_send.at[1], recv_sem=halo_recv.at[1],
-        device_id={"normal": lax.rem(z + z_count - 1, z_count)}, device_id_type=MESH,
-    )
-    pl.when(has_up)(upward.start)
-    pl.when(has_down)(downward.start)
-    exchange(send_m, recv_m, 0)
-
     def inner(t):
         @pl.when(t >= 8)
         def _():
@@ -382,7 +383,8 @@
         return jnp.where(low, roll_rows(plane, -1), roll_rows(plane, 1))
 
     for cell in range(4):
-        q = [halo[p, cell] for p in range(5)]
+        between = jnp.zeros((4, 128), jnp.float32)
+        q = [jnp.concatenate([halo[0, p, cell], between, halo[1, p, cell]], axis=0) for p in range(5)]
         flux = flux_of([jnp.where(q[0] > 0.0, q[0], 1.0)] + q[1:])
         factor = 32.0 + jnp.where(low, vis[cell, pl.ds(0, 8), :], vis[cell, pl.ds(8, 8), :])
         for p in range(5):
@@ -396,14 +398,14 @@
             for end in range(2):
                 send_r[pl.ds((28 * end + h) * R + p, 2, stride=2 * R), :] = rows[14 * end : 14 * end + 2]
 
-    def outer(t, carry):
+    def outer(t):
         @pl.when(t != me)
         def _():
             send_to(send_r, recv_r, 1, t)
 
-        return carry
-
-    lax.fori_loop(0, 8, outer, 0)
+    for dy in (2, 1, 3, 0):
+        for dc in (1, 0):
+            outer(along_y[dy] + cores[dc])
     own_copy(send_r, recv_r, 1).start()
 
     def get(recv, row, e):
@@ -444,13 +446,15 @@
                 l1[i + 1, r, 5 + c] = -upper[c]
         return carry
 
-    lax.fori_loop(0, 4, level_1, 0)
+    for i in range(4):
+        level_1(i, 0)
 
     def level_2_normalise(i, carry):
         normalise(d1, l1, 2 * i + 2)
         return carry
 
-    lax.fori_loop(0, 2, level_2_normalise, 0)
+    for i in range(2):
+        level_2_normalise(i, 0)
     for r in range(5):
         l1[0, r] = previous(l1[4, r], 1)
 
@@ -462,7 +466,8 @@
         combine(rows_of(l1, s), rows_of(d1, s), rows_of(l1, s - 1), rows_of(l1, s + 1), d2, l2, i)
         return carry
 
-    lax.fori_loop(0, 2, level_2_combine, 0)
+    for i in range(2):
+        level_2_combine(i, 0)
 
     normalise(d2, l2, 1)
     combine(
@@ -544,7 +549,8 @@
             pltpu.VMEM((4, 16, 128), f32),
             pltpu.VMEM((5, 4, 16, 128), f32),
             pltpu.VMEM((4, 5, 16, 128), f32),
-            pltpu.VMEM((5, 4, 8, 128), f32),
+            pltpu.VMEM((2, 5, 4, 2, 128), f32),
+            pltpu.VMEM((2, 5, 4, 2, 128), f32),
             pltpu.VMEM((5, 32, 128), f32),
         ]
         + [buffer, buffer, pltpu.VMEM((3 * N * R // 2, 128), f32), buffer, buffer, buffer]

time: 21.8 us -> 20.4 us (0.936)
  the two profiles are of different devices: /device:TPU:103 before, /device:TPU:1 now
where the time goes in v4:
time: 20.4 us
  Pallas kernels  19.7 us (97%)
  local copies, waits for them, and re-layouts  0.67 us (3%)
    pallas_call x1, Pallas kernels, on_device(): pl.pallas_call(kernel, out_shape=jax.ShapeDtypeStruct(state.shape, f32),...  19.7 us
    unnamed x1, local copies, waits for them, and re-layouts  0.67 us

profile of v4, /device:TPU:1, one launch (start us, length us, event | category | flops | bytes accessed | tf_op | source)
XLA Modules:
  0.0 20.4 jit_solution(10153788620141286824)
XLA Ops:
  0.0 19.7 %shard_map.37 = f32[5,4,16,128]{3,2,1,0:T(8,128)S(1)} custom-call(f32[5,4,16,128]{3,2,1,0:T(8,128)} %state_ref.1, f32[4,16,128]{2,1,0:T(8,128)} %visc_ref.1, f32[5,4,16,128]{3,2,1,0:T(8,128)} %resid_ref.1), custom_call_target="tpu_custom_call" | custom-call | tf_op jit(solution)/shard_map/pallas_call | solution.py:542
  19.7 0.7 %copy.5 = f32[5,4,16,128]{3,2,1,0:T(8,128)} copy(f32[5,4,16,128]{3,2,1,0:T(8,128)S(1)} %shard_map.37) | data formatting | bytes 327680

commit v5 on v4

--- a/solution.py
+++ b/solution.py
@@ -162,12 +162,15 @@
     return solve_rows(*factor_rows(rows), identity(rows[0][0]))
 
 
-def normalise(d_ref, x_ref, s):
+def normalise(d_ref, x_ref, s, keep=True):
     rows = [d_ref[s, r] for r in range(5)]
     unit = identity(rows[0][0])
-    x = solve_rows(*factor_rows(rows), [jnp.concatenate([x_ref[s, r], unit[r]], axis=0) for r in range(5)])
+    right = [jnp.concatenate([x_ref[s, r], unit[r]], axis=0) if keep else x_ref[s, r] for r in range(5)]
+    x = solve_rows(*factor_rows(rows), right)
     for r in range(5):
-        x_ref[s, r], d_ref[s, r] = x[r][:10], x[r][10:]
+        x_ref[s, r] = x[r][:10]
+        if keep:
+            d_ref[s, r] = x[r][10:]
 
 
 def times(rows, m):
@@ -201,6 +204,23 @@
     z = lax.axis_index("normal")
     z_count = lax.axis_size("normal")
 
+    has_up, has_down = z < z_count - 1, z > 0
+    along_x = [lax.rem(me // 8 + d, 4) * 8 for d in range(4)]
+    along_y = [lax.rem(lax.rem(me // 2, 4) + d, 4) * 2 for d in range(4)]
+    cores = [lax.rem(me, 2), 1 - lax.rem(me, 2)]
+    steps = [(dx, dy, dc) for dx in range(4) for dy in range(4) for dc in (1, 0) if dx or dy or dc]
+    steps.sort(key=lambda d: -(min(d[0], 4 - d[0]) + min(d[1], 4 - d[1])))
+
+    def for_partners(action, first=0, last=N):
+        for dx, dy, dc in steps[first:last]:
+            action(along_x[dx] + along_y[dy] + cores[dc])
+
+    barrier = pltpu.get_barrier_semaphore()
+
+    def greet(t):
+        pl.semaphore_signal(barrier, inc=1, device_id={"stream": t}, device_id_type=MESH)
+
+    for_partners(greet, 0, 10)
     def load(k, source, target):
         return pltpu.make_async_copy(source, target, in_sem.at[k])
 
@@ -213,19 +233,6 @@
         each.start()
 
     halo[...] = jnp.zeros_like(halo)
-    has_up, has_down = z < z_count - 1, z > 0
-    along_x = [lax.rem(me // 8 + d, 4) * 8 for d in range(4)]
-    along_y = [lax.rem(lax.rem(me // 2, 4) + d, 4) * 2 for d in range(4)]
-    cores = [lax.rem(me, 2), 1 - lax.rem(me, 2)]
-    steps = [(dx, dy, dc) for dx in range(4) for dy in range(4) for dc in (1, 0) if dx or dy or dc]
-    steps.sort(key=lambda d: -(min(d[0], 4 - d[0]) + min(d[1], 4 - d[1])))
-
-    def for_partners(action):
-        for dx, dy, dc in steps:
-            action(along_x[dx] + along_y[dy] + cores[dc])
-
-    barrier = pltpu.get_barrier_semaphore()
-
     @pl.when(has_up)
     def _():
         pl.semaphore_signal(barrier, inc=1, device_id={"normal": z + 1}, device_id_type=MESH)
@@ -234,7 +241,7 @@
     def _():
         pl.semaphore_signal(barrier, inc=1, device_id={"normal": z - 1}, device_id_type=MESH)
 
-    for_partners(lambda t: pl.semaphore_signal(barrier, inc=1, device_id={"stream": t}, device_id_type=MESH))
+    for_partners(greet, 10)
     for ends in (pl.ds(0, 8), pl.ds(24, 8)):
         st[:, :, ends, :] = jnp.zeros((5, 4, 8, 128), jnp.float32)
         gg[:, ends, :] = jnp.zeros((5, 8, 128), jnp.float32)
@@ -450,7 +457,7 @@
         level_1(i, 0)
 
     def level_2_normalise(i, carry):
-        normalise(d1, l1, 2 * i + 2)
+        normalise(d1, l1, 2 * i + 2, keep=False)
         return carry
 
     for i in range(2):

time: 20.4 us -> 20.3 us (level)
  no operation moved by 1% of the time
where the time goes in v5:
time: 20.3 us; the launch traced here: 20.2 us
  Pallas kernels  19.5 us (96%)
  local copies, waits for them, and re-layouts  0.67 us (3%)
    pallas_call x1, Pallas kernels, on_device(): pl.pallas_call(kernel, out_shape=jax.ShapeDtypeStruct(state.shape, f32),...  19.5 us
    unnamed x1, local copies, waits for them, and re-layouts  0.67 us

profile of v5, /device:TPU:1, one launch (start us, length us, event | category | flops | bytes accessed | tf_op | source)
XLA Modules:
  0.0 20.2 jit_solution(1673191630537256178)
XLA Ops:
  0.0 19.5 %shard_map.37 = f32[5,4,16,128]{3,2,1,0:T(8,128)S(1)} custom-call(f32[5,4,16,128]{3,2,1,0:T(8,128)} %state_ref.1, f32[4,16,128]{2,1,0:T(8,128)} %visc_ref.1, f32[5,4,16,128]{3,2,1,0:T(8,128)} %resid_ref.1), custom_call_target="tpu_custom_call" | custom-call | tf_op jit(solution)/shard_map/pallas_call | solution.py:549
  19.5 0.7 %copy.5 = f32[5,4,16,128]{3,2,1,0:T(8,128)} copy(f32[5,4,16,128]{3,2,1,0:T(8,128)S(1)} %shard_map.37) | data formatting | bytes 327680

commit v6 on v5

--- a/solution.py
+++ b/solution.py
@@ -34,16 +34,16 @@
 def previous(x, by):
     q, b = place(x.shape)
     if by == 1:
-        moved = roll_lanes(jnp.where(b, roll_rows(x, 1), x))
-        return jnp.where((q == 0) & ~b, 0.0, moved)
+        other = roll_lanes(x)
+        return jnp.where(b, other, jnp.where(q == 0, 0.0, roll_rows(other, 1)))
     return jnp.where(q < by // 2, 0.0, roll_rows(x, by // 2))
 
 
 def following(x, by):
     q, b = place(x.shape)
     if by == 1:
-        moved = roll_lanes(jnp.where(b, x, roll_rows(x, -1)))
-        return jnp.where((q == 7) & b, 0.0, moved)
+        other = roll_lanes(x)
+        return jnp.where(b, jnp.where(q == 7, 0.0, roll_rows(other, -1)), other)
     return jnp.where(q >= 8 - by // 2, 0.0, roll_rows(x, -(by // 2)))
 
 
@@ -232,7 +232,7 @@
     for each in loads:
         each.start()
 
-    halo[...] = jnp.zeros_like(halo)
+    halo[pl.ds(0, 2)] = jnp.zeros((2, 5, 4, 2, 128), jnp.float32)
     @pl.when(has_up)
     def _():
         pl.semaphore_signal(barrier, inc=1, device_id={"normal": z + 1}, device_id_type=MESH)
@@ -556,8 +556,8 @@
             pltpu.VMEM((4, 16, 128), f32),
             pltpu.VMEM((5, 4, 16, 128), f32),
             pltpu.VMEM((4, 5, 16, 128), f32),
-            pltpu.VMEM((2, 5, 4, 2, 128), f32),
-            pltpu.VMEM((2, 5, 4, 2, 128), f32),
+            pltpu.VMEM((3, 5, 4, 2, 128), f32),
+            pltpu.VMEM((3, 5, 4, 2, 128), f32),
             pltpu.VMEM((5, 32, 128), f32),
         ]
         + [buffer, buffer, pltpu.VMEM((3 * N * R // 2, 128), f32), buffer, buffer, buffer]

time: 20.3 us -> 20.3 us (level)
  no operation moved by 1% of the time
where the time goes in v6:
time: 20.3 us; the launch traced here: 20.2 us
  Pallas kernels  19.5 us (96%)
  local copies, waits for them, and re-layouts  0.67 us (3%)
    pallas_call x1, Pallas kernels, on_device(): pl.pallas_call(kernel, out_shape=jax.ShapeDtypeStruct(state.shape, f32),...  19.5 us
    unnamed x1, local copies, waits for them, and re-layouts  0.67 us

profile of v6, /device:TPU:1, one launch (start us, length us, event | category | flops | bytes accessed | tf_op | source)
XLA Modules:
  0.0 20.2 jit_solution(16633268949847539462)
XLA Ops:
  0.0 19.5 %shard_map.37 = f32[5,4,16,128]{3,2,1,0:T(8,128)S(1)} custom-call(f32[5,4,16,128]{3,2,1,0:T(8,128)} %state_ref.1, f32[4,16,128]{2,1,0:T(8,128)} %visc_ref.1, f32[5,4,16,128]{3,2,1,0:T(8,128)} %resid_ref.1), custom_call_target="tpu_custom_call" | custom-call | tf_op jit(solution)/shard_map/pallas_call | solution.py:549
  19.5 0.7 %copy.5 = f32[5,4,16,128]{3,2,1,0:T(8,128)} copy(f32[5,4,16,128]{3,2,1,0:T(8,128)S(1)} %shard_map.37) | data formatting | bytes 327680

commit v7 on v6

--- a/solution.py
+++ b/solution.py
@@ -173,6 +173,21 @@
             d_ref[s, r] = x[r][10:]
 
 
+def normalised(diagonal, own):
+    unit = identity(diagonal[0][0])
+    x = solve_rows(*factor_rows(diagonal), [jnp.concatenate([own[r], unit[r]], axis=0) for r in range(5)])
+    return [row[10:] for row in x], [row[:10] for row in x]
+
+
+def combined(own, diagonal, before, after):
+    left = [row_times(row[:5], before) for row in own]
+    right = [row_times(row[5:], after) for row in own]
+    return (
+        [diagonal[r] - left[r][5:] - right[r][:5] for r in range(5)],
+        [jnp.concatenate([-left[r][:5], -right[r][5:]], axis=0) for r in range(5)],
+    )
+
+
 def times(rows, m):
     return [row_times(row, m) for row in rows]
 
@@ -197,7 +212,7 @@
 def kernel(
     state_ref, visc_ref, resid_ref, out_ref,
     st, vis, res, ro, halo, away, gg, send_m, recv_m, send_r, recv_r, send_x, recv_x,
-    prm, d1, l1, d2, l2, dp, lp,
+    prm, d1, l1, d2, l2,
     in_sem, halo_send, halo_recv, a2a_send, a2a_recv, own_sem,
 ):
     me = lax.axis_index("stream")
@@ -476,22 +491,21 @@
     for i in range(2):
         level_2_combine(i, 0)
 
-    normalise(d2, l2, 1)
-    combine(
-        rows_of(l2, 0), rows_of(d2, 0), [previous(l2[1, r], 1) for r in range(5)], rows_of(l2, 1), dp, lp, 0
-    )
+    inverse_4, own_4 = normalised(rows_of(d2, 1), rows_of(l2, 1))
+    own_0 = rows_of(l2, 0)
+    diagonal, own = combined(own_0, rows_of(d2, 0), [previous(row, 1) for row in own_4], own_4)
 
     unit = identity(jnp.ones((8, 128), jnp.float32))
+    levels = []
     for step in range(3):
-        normalise(dp, lp, step)
-        own = rows_of(lp, step)
-        combine(
-            own, unit, [previous(x, 2**step) for x in own], [following(x, 2**step) for x in own],
-            dp, lp, step + 1,
+        inverse, own = normalised(diagonal, own)
+        levels.append((inverse, own))
+        diagonal, own = combined(
+            own, unit, [previous(x, 2**step) for x in own], [following(x, 2**step) for x in own]
         )
     q, _ = place((5, 8, 128))
-    other = [jnp.where(q < 4, lp[3, r, pl.ds(5, 5)], lp[3, r, pl.ds(0, 5)]) for r in range(5)]
-    both = solve_rows(*factor_rows(rows_of(dp, 3)), [jnp.concatenate([other[r], unit[r]], axis=0) for r in range(5)])
+    other = [jnp.where(q < 4, own[r][5:], own[r][:5]) for r in range(5)]
+    both = solve_rows(*factor_rows(diagonal), [jnp.concatenate([other[r], unit[r]], axis=0) for r in range(5)])
     other, fourth = [row[:5] for row in both], [row[5:] for row in both]
     facing = [roll_rows(x, 4) for x in other]
     last = inverse_of([unit[r] - row_times(other[r], facing) for r in range(5)])
@@ -504,20 +518,20 @@
         t = shifted(gas(i + 1), before, prm[5, i + 2])
         four[i] = [parts[i // 4][p][0] + t[p] for p in range(5)]
     y = {}
-    y[4] = times(rows_of(d2, 1), four[4])
+    y[4] = times(inverse_4, four[4])
     before = [previous(value, 1) for value in y[4]]
-    b = [subtract(l2[0, r], four[0][r], before, y[4]) for r in range(5)]
+    b = [subtract(own_0[r], four[0][r], before, y[4]) for r in range(5)]
     for step in range(3):
-        b = times(rows_of(dp, step), b)
+        b = times(levels[step][0], b)
         before = [previous(value, 2**step) for value in b]
         after = [following(value, 2**step) for value in b]
-        b = [subtract(lp[step, r], b[r], before, after) for r in range(5)]
+        b = [subtract(levels[step][1][r], b[r], before, after) for r in range(5)]
     b = times(fourth, b)
     paired = [roll_rows(value, 4) for value in b]
     b = [b[r] - row_times(other[r], paired) for r in range(5)]
     x = {0: times(last, b)}
     x[8] = [following(value, 1) for value in x[0]]
-    x[4] = [subtract(l2[1, r], y[4][r], x[0], x[8]) for r in range(5)]
+    x[4] = [subtract(own_4[r], y[4][r], x[0], x[8]) for r in range(5)]
 
     for e in range(2):
         beyond = shifted(gas(4 * e + 6), x[4 * e + 4], -prm[5, 4 * e + 5])
@@ -567,8 +581,6 @@
             pltpu.VMEM((5, 5, 10) + tile, f32),
             pltpu.VMEM((2, 5, 5) + tile, f32),
             pltpu.VMEM((2, 5, 10) + tile, f32),
-            pltpu.VMEM((4, 5, 5) + tile, f32),
-            pltpu.VMEM((4, 5, 10) + tile, f32),
             pltpu.SemaphoreType.DMA((3,)),
             pltpu.SemaphoreType.DMA((2,)),
             pltpu.SemaphoreType.DMA((2,)),

time: 20.3 us -> 20.3 us (level)
  no operation moved by 1% of the time
where the time goes in v7:
time: 20.3 us; the launch traced here: 20.2 us
  Pallas kernels  19.5 us (96%)
  local copies, waits for them, and re-layouts  0.67 us (3%)
    pallas_call x1, Pallas kernels, on_device(): pl.pallas_call(kernel, out_shape=jax.ShapeDtypeStruct(state.shape, f32),...  19.5 us
    unnamed x1, local copies, waits for them, and re-layouts  0.67 us

profile of v7, /device:TPU:1, one launch (start us, length us, event | category | flops | bytes accessed | tf_op | source)
XLA Modules:
  0.0 20.2 jit_solution(9771027895681746361)
XLA Ops:
  0.0 19.5 %shard_map.37 = f32[5,4,16,128]{3,2,1,0:T(8,128)S(1)} custom-call(f32[5,4,16,128]{3,2,1,0:T(8,128)} %state_ref.1, f32[4,16,128]{2,1,0:T(8,128)} %visc_ref.1, f32[5,4,16,128]{3,2,1,0:T(8,128)} %resid_ref.1), custom_call_target="tpu_custom_call" | custom-call | tf_op jit(solution)/shard_map/pallas_call | solution.py:563
  19.5 0.7 %copy.5 = f32[5,4,16,128]{3,2,1,0:T(8,128)} copy(f32[5,4,16,128]{3,2,1,0:T(8,128)S(1)} %shard_map.37) | data formatting | bytes 327680

commit v8 on v6

--- a/solution.py
+++ b/solution.py
@@ -307,6 +307,57 @@
             put(send_m, 2 * p + c, gas_own[c][p], gas_own[c + 2][p])
         put(send_m, 8 + c, sig[c], sig[c + 2])
 
+    def flux_of(q):
+        rho, m1, m2, m3, energy = q
+        inverse = 1.0 / rho
+        pressure = 0.4 * (energy - 0.5 * (m1 * m1 + m2 * m2 + m3 * m3) * inverse)
+        v = m2 * inverse
+        return [m2, m1 * v, m2 * v + pressure, m3 * v, (energy + pressure) * v]
+
+    loads[2].wait()
+    for cell in range(4):
+        flux = flux_of([st[p, cell, pl.ds(8, 16), :] for p in range(5)])
+        for p in range(5):
+            gg[p, pl.ds(8, 16)] = flux[p]
+            s = {d: st[p, cell, pl.ds(8 + d, 16), :] for d in (-2, -1, 0, 1, 2)}
+            g = {d: gg[p, pl.ds(8 + d, 16), :] for d in (-1, 1)}
+            ro[cell, p] = (
+                res[p, cell]
+                - 40.0 * (g[1] - g[-1])
+                + vis[cell] * (s[1] - 2.0 * s[0] + s[-1])
+                - 8.0 * (s[2] - 4.0 * s[1] + 6.0 * s[0] - 4.0 * s[-1] + s[-2])
+            )
+
+    inv1, inv3 = (1.0 / (1.0 + 2.0 * sig[cell]) for cell in (1, 3))
+    own_inverse = inverse_of([
+        jnp.stack(values)
+        for values in diagonal_rows(
+            scaled(jacobian_rows(*gas_own[1]), sig[2], inv1), scaled(jacobian_rows(*gas_own[3]), -sig[2], inv3),
+            gas_own[2], sig[1], sig[2], sig[3],
+        )
+    ])
+
+    def around(y1, x2, y3):
+        flux = jacobian_times(gas_own[2], x2)
+        x1 = [y1[p] - inv1 * (flux[p] - sig[1] * x2[p]) for p in range(5)]
+        return x1, [y3[p] + inv3 * (flux[p] + sig[3] * x2[p]) for p in range(5)]
+
+    def to_cell_2(y1, y3):
+        a, b = shifted(gas_own[1], y1, sig[2]), shifted(gas_own[3], y3, -sig[2])
+        return [a[p] - b[p] for p in range(5)]
+
+    def condensed():
+        y1, y3 = [inv1 * ro[1, p] for p in range(5)], [inv3 * ro[3, p] for p in range(5)]
+        t = to_cell_2(y1, y3)
+        x2 = times(own_inverse, [ro[2, p] + t[p] for p in range(5)])
+        x1, x3 = around(y1, x2, y3)
+        t = shifted(gas_own[1], x1, -sig[0])
+        return [ro[0, p] - t[p] for p in range(5)], x3, y1, x2, y3
+
+    rest, x3, *_ = condensed()
+    for p in range(5):
+        put(send_r, p, rest[p], x3[p])
+
     pl.semaphore_wait(barrier, N - 1 + has_up.astype(jnp.int32) + has_down.astype(jnp.int32))
     upward = pltpu.make_async_remote_copy(
         src_ref=away.at[0], dst_ref=halo.at[0],
@@ -321,57 +372,6 @@
     pl.when(has_up)(upward.start)
     pl.when(has_down)(downward.start)
     exchange(send_m, recv_m, 0)
-
-    def flux_of(q):
-        rho, m1, m2, m3, energy = q
-        inverse = 1.0 / rho
-        pressure = 0.4 * (energy - 0.5 * (m1 * m1 + m2 * m2 + m3 * m3) * inverse)
-        v = m2 * inverse
-        return [m2, m1 * v, m2 * v + pressure, m3 * v, (energy + pressure) * v]
-
-    loads[2].wait()
-    for cell in range(4):
-        flux = flux_of([st[p, cell, pl.ds(8, 16), :] for p in range(5)])
-        for p in range(5):
-            gg[p, pl.ds(8, 16)] = flux[p]
-            s = {d: st[p, cell, pl.ds(8 + d, 16), :] for d in (-2, -1, 0, 1, 2)}
-            g = {d: gg[p, pl.ds(8 + d, 16), :] for d in (-1, 1)}
-            ro[cell, p] = (
-                res[p, cell]
-                - 40.0 * (g[1] - g[-1])
-                + vis[cell] * (s[1] - 2.0 * s[0] + s[-1])
-                - 8.0 * (s[2] - 4.0 * s[1] + 6.0 * s[0] - 4.0 * s[-1] + s[-2])
-            )
-
-    inv1, inv3 = (1.0 / (1.0 + 2.0 * sig[cell]) for cell in (1, 3))
-    own_inverse = inverse_of([
-        jnp.stack(values)
-        for values in diagonal_rows(
-            scaled(jacobian_rows(*gas_own[1]), sig[2], inv1), scaled(jacobian_rows(*gas_own[3]), -sig[2], inv3),
-            gas_own[2], sig[1], sig[2], sig[3],
-        )
-    ])
-
-    def around(y1, x2, y3):
-        flux = jacobian_times(gas_own[2], x2)
-        x1 = [y1[p] - inv1 * (flux[p] - sig[1] * x2[p]) for p in range(5)]
-        return x1, [y3[p] + inv3 * (flux[p] + sig[3] * x2[p]) for p in range(5)]
-
-    def to_cell_2(y1, y3):
-        a, b = shifted(gas_own[1], y1, sig[2]), shifted(gas_own[3], y3, -sig[2])
-        return [a[p] - b[p] for p in range(5)]
-
-    def condensed():
-        y1, y3 = [inv1 * ro[1, p] for p in range(5)], [inv3 * ro[3, p] for p in range(5)]
-        t = to_cell_2(y1, y3)
-        x2 = times(own_inverse, [ro[2, p] + t[p] for p in range(5)])
-        x1, x3 = around(y1, x2, y3)
-        t = shifted(gas_own[1], x1, -sig[0])
-        return [ro[0, p] - t[p] for p in range(5)], x3, y1, x2, y3
-
-    rest, x3, *_ = condensed()
-    for p in range(5):
-        put(send_r, p, rest[p], x3[p])
 
     def inner(t):
         @pl.when(t >= 8)

time: 20.3 us -> 20.3 us (level)
  no operation moved by 1% of the time
where the time goes in v8:
time: 20.3 us; the launch traced here: 20.2 us
  Pallas kernels  19.5 us (96%)
  local copies, waits for them, and re-layouts  0.67 us (3%)
    pallas_call x1, Pallas kernels, on_device(): pl.pallas_call(kernel, out_shape=jax.ShapeDtypeStruct(state.shape, f32),...  19.5 us
    unnamed x1, local copies, waits for them, and re-layouts  0.67 us

profile of v8, /device:TPU:1, one launch (start us, length us, event | category | flops | bytes accessed | tf_op | source)
XLA Modules:
  0.0 20.2 jit_solution(16903501081479346384)
XLA Ops:
  0.0 19.5 %shard_map.37 = f32[5,4,16,128]{3,2,1,0:T(8,128)S(1)} custom-call(f32[5,4,16,128]{3,2,1,0:T(8,128)} %state_ref.1, f32[4,16,128]{2,1,0:T(8,128)} %visc_ref.1, f32[5,4,16,128]{3,2,1,0:T(8,128)} %resid_ref.1), custom_call_target="tpu_custom_call" | custom-call | tf_op jit(solution)/shard_map/pallas_call | solution.py:549
  19.5 0.7 %copy.5 = f32[5,4,16,128]{3,2,1,0:T(8,128)} copy(f32[5,4,16,128]{3,2,1,0:T(8,128)S(1)} %shard_map.37) | data formatting | bytes 327680
